TPU v7x, 256 devices: a whole 4x4x8 slice. The times are simulated.
256 devices in a mesh: ctx: 16 (over z_lo, x, core), exp: 16 (over z_hi, y).
Axes of the slice: x: 4, y: 4, z: 8 (z_hi: 4, z_lo: 2; z = z_hi * 2 + z_lo), core: 2. Of those that a mesh axis runs over, the one named last changes fastest.
Arguments:
- queries: bfloat16 [16, 2048, 1536], P('exp', 'ctx'), may hold values from -2.5 to 2.5
- key_states: bfloat16 [16, 2048, 1536], P('exp', 'ctx'), may hold values from -2.5 to 2.5
- value_states: bfloat16 [16, 2048, 1536], P('exp', 'ctx'), may hold values from -6 to 6
- attended: bfloat16 [16, 2048, 1536], P('exp', 'ctx'), may hold values from -6 to 6
- output_grad: bfloat16 [16, 2048, 1536], P('exp', 'ctx'), may hold values from -6 to 6
- expert_ids: int32 [16, 2048, 2], P('exp', 'ctx'), may hold values from 0 to 15, all different within a row; in each aligned block of 128 rows (0 to 127, 128 to 255, ..., all dimensions but the last counted through in order) at most 24 rows name the same one
- gate_weights: float32 [16, 2048, 2], P('exp', 'ctx'), may hold values from 0.2 to 1
- w_in: bfloat16 [16, 1536, 768], P('exp'), may hold values from -0.15625 to 0.15625
- w_out: bfloat16 [16, 768, 1536], P('exp'), may hold values from -0.21875 to 0.21875
Outputs:
- query_grad: bfloat16 [16, 2048, 1536], P('exp', 'ctx')
- key_grad: bfloat16 [16, 2048, 1536], P('exp', 'ctx')
- value_grad: bfloat16 [16, 2048, 1536], P('exp', 'ctx')
- w_in_grad: bfloat16 [16, 1536, 768], P('exp', 'ctx')
- w_out_grad: bfloat16 [16, 768, 1536], P('exp', 'ctx')
Inputs may be any that keep to these rules, and one draw needn't show every extreme that they name: `expert_ids`: in each aligned block of 128 frames (the frames of one device) no expert is named by more than 24 frames, a bound that some block reaches; the two experts of a frame differ.
All inputs are finite; a program needn't handle non-finite values.
Results may differ from a plain program's by a relative error of at most 0.02.
Values may be sent and summed in bfloat16 or wider, within the bound.
A program may use at most 128 MiB of HBM per device.

v0:
```python
import jax
import jax.numpy as jnp
from jax import lax
from jax.sharding import PartitionSpec as P

HEAD_DIM = 128
EXP_DEV = 1


def rounded(x):
    return lax.optimization_barrier(x.astype(jnp.bfloat16)).astype(jnp.float32)


def per_device(
    queries, key_states, value_states, attended, output_grad, expert_ids, gate_weights, w_in, w_out
):
    tok = queries.shape[1]
    width = queries.shape[2]
    heads = width // HEAD_DIM
    nexp = lax.axis_size("exp")
    nctx = lax.axis_size("ctx")
    experts = EXP_DEV * nexp
    capacity = 3 * tok // experts
    attn_rows = attended[0]
    grad_rows = output_grad[0]
    route = expert_ids[0].reshape(-1)
    gates = gate_weights[0].reshape(-1)
    onehot = (route[:, None] == jnp.arange(experts, dtype=jnp.int32)[None, :]).astype(jnp.int32)
    slots = jnp.sum((jnp.cumsum(onehot, axis=0) - 1) * onehot, axis=1)
    target = route * capacity + slots
    placed = target[None, :] == jnp.arange(experts * capacity, dtype=jnp.int32)[:, None]
    picker = (
        placed.reshape(experts * capacity, tok, 2)
        .astype(jnp.float32)
        .sum(axis=2)
        .astype(jnp.bfloat16)
    )
    slot_gate = jnp.sum(jnp.where(placed, gates[None, :], 0.0), axis=1)
    sent_rows = jnp.dot(picker, attn_rows, preferred_element_type=jnp.float32).astype(jnp.bfloat16)
    sent_grads = (
        jnp.dot(picker, grad_rows, preferred_element_type=jnp.float32) * slot_gate[:, None]
    ).astype(jnp.bfloat16)
    shape = (nexp, EXP_DEV * capacity, width)
    got_rows, got_grads = (
        lax.all_to_all(sent_rows.reshape(shape), "exp", split_axis=0, concat_axis=0, tiled=True),
        lax.all_to_all(sent_grads.reshape(shape), "exp", split_axis=0, concat_axis=0, tiled=True),
    )

    def by_expert(values):
        return (
            values.reshape(nexp, EXP_DEV, capacity, -1)
            .transpose(1, 0, 2, 3)
            .reshape(EXP_DEV, nexp * capacity, -1)
        )

    rows_in = by_expert(got_rows)
    grads_in = by_expert(got_grads)
    upper = jnp.einsum("erd,edf->erf", rows_in, w_in, preferred_element_type=jnp.float32)
    sig = jax.nn.sigmoid(upper)
    act = (upper * sig).astype(jnp.bfloat16)
    act_grad = jnp.einsum("erd,efd->erf", grads_in, w_out, preferred_element_type=jnp.float32)
    up_grad = (act_grad * sig * (1.0 + upper * (1.0 - sig))).astype(jnp.bfloat16)
    row_back = jnp.einsum("erf,edf->erd", up_grad, w_in, preferred_element_type=jnp.float32).astype(
        jnp.bfloat16
    )
    first_term = jnp.einsum("erd,erf->edf", rows_in, up_grad, preferred_element_type=jnp.float32)
    second_term = jnp.einsum("erf,erd->efd", act, grads_in, preferred_element_type=jnp.float32)
    back_send = (
        row_back.reshape(EXP_DEV, nexp, capacity, width).transpose(1, 0, 2, 3).reshape(shape)
    )
    returned = lax.all_to_all(back_send, "exp", split_axis=0, concat_axis=0, tiled=True)
    back_sum = jnp.dot(
        picker.T, returned.reshape(experts * capacity, width), preferred_element_type=jnp.float32
    )
    attn_grad = (grad_rows.astype(jnp.float32) + back_sum).astype(jnp.bfloat16)
    first_sum, second_sum = (
        lax.psum_scatter(
            first_term.astype(jnp.bfloat16), "ctx", scatter_dimension=1, tiled=True
        ).astype(jnp.float32),
        lax.psum_scatter(
            second_term.astype(jnp.bfloat16), "ctx", scatter_dimension=1, tiled=True
        ).astype(jnp.float32),
    )
    w_in_grad = first_sum.astype(jnp.bfloat16)
    w_out_grad = second_sum.astype(jnp.bfloat16)
    scale = HEAD_DIM ** (-0.5)
    group = min(max(1, 512 // tok), nctx)
    blocks = nctx // group
    query_heads = queries[0].reshape(tok, heads, HEAD_DIM)
    grad_heads = attn_grad.reshape(tok, heads, HEAD_DIM)
    delta = jnp.sum(
        (attn_grad.astype(jnp.float32) * attn_rows.astype(jnp.float32)).reshape(
            tok, heads, HEAD_DIM
        ),
        axis=2,
    )
    key_all, value_all = (
        lax.all_gather(key_states[0], "ctx", axis=0, tiled=True),
        lax.all_gather(value_states[0], "ctx", axis=0, tiled=True),
    )
    key_blocks = key_all.reshape(blocks, group, tok, heads, HEAD_DIM)
    value_blocks = value_all.reshape(blocks, group, tok, heads, HEAD_DIM)

    def norm_step(total, key_blk):
        scores = (
            jnp.einsum("qhd,gkhd->hqgk", query_heads, key_blk, preferred_element_type=jnp.float32)
            * scale
        )
        return (total + jnp.sum(jnp.exp(scores), axis=(2, 3)), None)

    totals, _ = lax.scan(norm_step, jnp.zeros((heads, tok), jnp.float32), key_blocks)
    norm_log = jnp.log(totals)

    def grad_step(query_acc, blk):
        key_blk, value_blk = blk
        scores = (
            jnp.einsum("qhd,gkhd->hqgk", query_heads, key_blk, preferred_element_type=jnp.float32)
            * scale
        )
        probs = jnp.exp(scores - norm_log[:, :, None, None])
        probs_b = probs.astype(jnp.bfloat16)
        prob_grad = jnp.einsum(
            "qhd,gkhd->hqgk", grad_heads, value_blk, preferred_element_type=jnp.float32
        )
        score_grad = (probs * (prob_grad - delta.T[:, :, None, None])).astype(jnp.bfloat16)
        query_part = (
            jnp.einsum("hqgk,gkhd->gqhd", score_grad, key_blk, preferred_element_type=jnp.float32)
            * scale
        )
        query_acc = query_acc + jnp.sum(rounded(query_part), axis=0)
        key_term = (
            jnp.einsum(
                "hqgk,qhd->gkhd", score_grad, query_heads, preferred_element_type=jnp.float32
            )
            * scale
        )
        value_term = jnp.einsum(
            "hqgk,qhd->gkhd", probs_b, grad_heads, preferred_element_type=jnp.float32
        )
        return (query_acc, (key_term, value_term))

    query_acc, (key_terms, value_terms) = lax.scan(
        grad_step, jnp.zeros((tok, heads, HEAD_DIM), jnp.float32), (key_blocks, value_blocks)
    )
    key_sum, value_sum = (
        lax.psum_scatter(
            key_terms.reshape(nctx * tok, width).astype(jnp.bfloat16),
            "ctx",
            scatter_dimension=0,
            tiled=True,
        ).astype(jnp.float32),
        lax.psum_scatter(
            value_terms.reshape(nctx * tok, width).astype(jnp.bfloat16),
            "ctx",
            scatter_dimension=0,
            tiled=True,
        ).astype(jnp.float32),
    )
    query_grad = query_acc.reshape(tok, width).astype(jnp.bfloat16)
    key_grad = key_sum.astype(jnp.bfloat16)
    value_grad = value_sum.astype(jnp.bfloat16)
    return (query_grad[None], key_grad[None], value_grad[None], w_in_grad, w_out_grad)


def solution(mesh):
    return jax.shard_map(
        per_device,
        mesh=mesh,
        in_specs=(
            P("exp", "ctx", None),
            P("exp", "ctx", None),
            P("exp", "ctx", None),
            P("exp", "ctx", None),
            P("exp", "ctx", None),
            P("exp", "ctx", None),
            P("exp", "ctx", None),
            P("exp", None, None),
            P("exp", None, None),
        ),
        out_specs=(
            P("exp", "ctx", None),
            P("exp", "ctx", None),
            P("exp", "ctx", None),
            P("exp", "ctx", None),
            P("exp", "ctx", None),
        ),
        check_vma=False,
    )
```

profile of v0, /device:TPU:1, one launch (start us, length us, event | category | flops | bytes accessed | tf_op | source)
XLA Modules:
  0.0 579.9 jit_solution(6639492510008456420)
XLA Ops:
  11.0 2.5 convolution_convert_fusion.2
  13.4 11.8 %all-to-all-start.1 = ((bf16[16,24,1536]{2,1,0:T(8,128)(2,1)}), bf16[16,24,1536]{2,1,0:T(8,128)(2,1)}, u32[]{:S(2)}, u32[]{:S(2)}) async-start(bf16[16,24,1536]{2,1,0:T(8,128)(2,1)} %bitcast.8), calls=%async_computation.1 | async-start | bytes 2359296 | tf_op jit(solution)/shard_map/all_to_all | solution.py:45
  25.7 1.5 fusion.30
  27.2 42.6 %all-to-all-done.1 = bf16[16,24,1536]{2,1,0:T(8,128)(2,1)} async-done(((bf16[16,24,1536]{2,1,0:T(8,128)(2,1)}), bf16[16,24,1536]{2,1,0:T(8,128)(2,1)}, u32[]{:S(2)}, u32[]{:S(2)}) %all-to-all-start.1) | async-done | bytes 1179680 | tf_op jit(solution)/shard_map/all_to_all | solution.py:45
  69.7 4.4 all-to-all-start
  74.2 3.4 fusion.33
  77.6 34.6 %all-to-all-done = bf16[16,24,1536]{2,1,0:T(8,128)(2,1)} async-done(((bf16[16,24,1536]{2,1,0:T(8,128)(2,1)}), bf16[16,24,1536]{2,1,0:T(8,128)(2,1)}, u32[]{:S(2)}, u32[]{:S(2)}) %all-to-all-start) | async-done | bytes 1179680 | tf_op jit(solution)/shard_map/all_to_all | solution.py:46
  112.1 3.7 fusion.43
  115.8 2.1 convolution_convert_fusion.3
  118.0 3.9 all-to-all-start.2
  122.6 43.5 %all-to-all-done.2 = bf16[16,24,1536]{2,1,0:T(8,128)(2,1)S(1)} async-done(((bf16[16,24,1536]{2,1,0:T(8,128)(2,1)}), bf16[16,24,1536]{2,1,0:T(8,128)(2,1)S(1)}, u32[]{:S(2)}, u32[]{:S(2)}) %all-to-all-start.2) | async-done | bytes 1179680 | tf_op jit(solution)/shard_map/all_to_all | solution.py:71
  166.1 2.3 convert_multiply_fusion
  168.7 1.2 copy.80
  170.3 12.2 %reshape.156 = bf16[4,4,128,12,128]{4,3,2,1,0:T(8,128)(2,1)} reshape(bf16[1,2048,1536]{2,1,0:T(8,128)(2,1)} %all-gather.7.cloned.1.call-done) | data formatting | bytes 12582912 | tf_op jit(solution)/shard_map/reshape | solution.py:102
  182.5 7.8 %copy.84 = bf16[4,4,128,12,128]{4,2,1,3,0:T(8,128)(2,1)} copy(bf16[4,4,128,12,128]{4,3,2,1,0:T(8,128)(2,1)} %reshape.156) | data formatting | bytes 12582912
  190.3 12.2 %reshape.161 = bf16[4,4,128,12,128]{4,3,2,1,0:T(8,128)(2,1)} reshape(bf16[1,2048,1536]{2,1,0:T(8,128)(2,1)} %all-gather.5.cloned.1.call-done) | data formatting | bytes 12582912 | tf_op jit(solution)/shard_map/reshape | solution.py:101
  202.5 7.7 %copy.82 = bf16[4,4,128,12,128]{4,2,1,3,0:T(8,128)(2,1)} copy(bf16[4,4,128,12,128]{4,3,2,1,0:T(8,128)(2,1)} %reshape.161) | data formatting | bytes 12582912
  210.2 8.3 %while.26 = (s32[]{:T(128)}, f32[12,128]{1,0:T(8,128)S(1)}, bf16[4,4,128,12,128]{4,2,1,3,0:T(8,128)(2,1)}, bf16[128,12,128]{2,0,1:T(8,128)(2,1)S(1)}, s32[]{:T(128)}, /*index=5*/s32[]{:T(128)}) while((s32[]{:T(128)}, f32[12,128]{1,0:T(8,128)S(1)}, bf16[4,4,128,12,128]{4,2,1,3,0:T(8,128)(2,1)}, bf16[128,12,128]{2,0,1:T(8,128)(2,1)S(1)}, ...), condition=%wide.region_2.3_spmd.clone, body=%wide.region_0.2_spmd.clone.sunk | while | flops 202900992 | bytes 1990747 | solution.py:111
  210.2 2.0 exponential_reduce_fusion.2
  212.2 2.0 exponential_reduce_fusion.2
  214.3 2.0 exponential_reduce_fusion.2
  216.4 2.0 exponential_reduce_fusion.2
  218.4 58.2 %while.27 = (s32[]{:T(128)}, f32[128,12,128]{0,2,1:T(8,128)S(1)}, bf16[4,4,128,12,128]{4,2,1,3,0:T(8,128)(2,1)}, bf16[4,4,128,12,128]{4,2,1,3,0:T(8,128)(2,1)}, ...) while((s32[]{:T(128)}, f32[128,12,128]{0,2,1:T(8,128)S(1)}, ...), condition=%wide.region_11.12_spmd.clone, body=%wide.region_9.11_spmd.clone.sunk | while | flops 1017053184 | bytes 121131312 | solution.py:142
  218.4 2.0 fusion.95
  220.4 2.5 fusion.96
  223.0 2.3 fusion.97
  226.7 1.0 slice-done.3
  228.4 1.9 copy-done.2
  230.3 2.6 copy-done.3
  232.9 2.0 fusion.95
  234.9 2.5 fusion.96
  237.4 2.3 fusion.97
  241.2 1.0 slice-done.3
  242.9 1.9 copy-done.2
  244.8 2.6 copy-done.3
  247.4 2.0 fusion.95
  249.4 2.5 fusion.96
  251.9 2.3 fusion.97
  255.7 1.0 slice-done.3
  257.4 1.9 copy-done.2
  259.3 2.6 copy-done.3
  261.9 2.0 fusion.95
  263.9 2.5 fusion.96
  266.4 2.3 fusion.97
  270.1 1.0 slice-done.3
  271.9 1.9 copy-done.2
  273.8 2.6 copy-done.3
  276.6 11.3 %copy.107 = bf16[4,4,128,12,128]{4,3,2,1,0:T(8,128)(2,1)} copy(bf16[4,4,128,12,128]{4,2,1,3,0:T(8,128)(2,1)} %get-tuple-element.84) | data formatting | bytes 12582912
  287.9 9.3 %copy.124 = bf16[256,8,12,128]{3,1,2,0:T(8,128)(2,1)} copy(bf16[256,8,12,128]{3,2,1,0:T(8,128)(2,1)} %bitcast.163) | data formatting | bytes 12582912
  297.6 11.3 %copy.106 = bf16[4,4,128,12,128]{4,3,2,1,0:T(8,128)(2,1)} copy(bf16[4,4,128,12,128]{4,2,1,3,0:T(8,128)(2,1)} %get-tuple-element.83) | data formatting | bytes 12582912
  308.9 9.3 %copy.125 = bf16[256,8,12,128]{3,1,2,0:T(8,128)(2,1)} copy(bf16[256,8,12,128]{3,2,1,0:T(8,128)(2,1)} %bitcast.164) | data formatting | bytes 12582912
  318.2 1.2 copy-done.7
  319.4 4.1 fusion.29
  323.7 1.0 copy-done.9
  324.7 4.1 fusion.28
  328.9 0.9 copy.88
  329.8 34.1 %reduce-scatter.15.cloned.1.call-done = bf16[128,1536]{1,0:T(8,128)(2,1)} async-done(((bf16[2048,1536]{1,0:T(8,128)(2,1)}), bf16[128,1536]{1,0:T(8,128)(2,1)}) %reduce-scatter.15.cloned.1.call-update) | async-done | bytes 393232
  363.9 1.2 copy.103
  365.1 0.9 copy.90
  366.0 71.6 %reduce-scatter.13.cloned.1.call-done = bf16[128,1536]{1,0:T(8,128)(2,1)} async-done(((bf16[2048,1536]{1,0:T(8,128)(2,1)}), bf16[128,1536]{1,0:T(8,128)(2,1)}) %reduce-scatter.13.cloned.1.call-update) | async-done | bytes 393232
  437.6 1.2 copy.101
  438.8 0.9 copy.89
  439.8 65.5 %reduce-scatter.11.cloned.1.call-done = bf16[1,48,1536]{2,1,0:T(8,128)(2,1)} async-done(((bf16[1,768,1536]{2,1,0:T(8,128)(2,1)}), bf16[1,48,1536]{2,1,0:T(8,128)(2,1)}) %reduce-scatter.11.cloned.1.call-update) | async-done | bytes 147472 | tf_op jit(solution)/shard_map/reduce_scatter | solution.py:80
  505.3 67.4 %reduce-scatter.9.cloned.1.call-done = bf16[1,96,768]{2,1,0:T(8,128)(2,1)} async-done(((bf16[1,1536,768]{2,1,0:T(8,128)(2,1)}), bf16[1,96,768]{2,1,0:T(8,128)(2,1)}) %reduce-scatter.9.cloned.1.call-update) | async-done | bytes 147472 | tf_op jit(solution)/shard_map/reduce_scatter | solution.py:77
  (120 shorter events, 14.4 us)
Async XLA Ops:
  7.2 67.0 %copy-start = (bf16[1,1536,768]{2,1,0:T(8,128)(2,1)S(1)}, bf16[1,1536,768]{2,1,0:T(8,128)(2,1)}, u32[]{:S(2)}) copy-start(bf16[1,1536,768]{2,1,0:T(8,128)(2,1)} %param.20) | copy-start | bytes 7077892
  7.2 163.1 %all-gather.7.cloned.1.call-start = ((), (), s32[]{:S(2)}) async-start(), calls=%async_computation.10 | async-start | bytes 6684672 | tf_op jit(solution)/shard_map/all_gather | solution.py:99
  7.9 182.4 %all-gather.5.cloned.1.call-start = ((), (), s32[]{:S(2)}) async-start(), calls=%async_computation.9 | async-start | bytes 6684672 | tf_op jit(solution)/shard_map/all_gather | solution.py:98
  9.5 15.8 %copy-start.6 = (f32[1,128,2]{1,2,0:T(2,128)S(1)}, f32[1,128,2]{1,2,0:T(2,128)}, u32[]{:S(2)}) copy-start(f32[1,128,2]{1,2,0:T(2,128)} %param.19) | copy-start | bytes 3076
  9.7 15.9 %copy-start.4 = (bf16[1,128,1536]{2,1,0:T(8,128)(2,1)S(1)}, bf16[1,128,1536]{2,1,0:T(8,128)(2,1)}, u32[]{:S(2)}) copy-start(bf16[1,128,1536]{2,1,0:T(8,128)(2,1)} %param.17) | copy-start | bytes 1179652
  13.4 56.3 %all-to-all-start.1 = ((bf16[16,24,1536]{2,1,0:T(8,128)(2,1)}), bf16[16,24,1536]{2,1,0:T(8,128)(2,1)}, u32[]{:S(2)}, u32[]{:S(2)}) async-start(bf16[16,24,1536]{2,1,0:T(8,128)(2,1)} %bitcast.8), calls=%async_computation.1 | async-start | bytes 2359296 | tf_op jit(solution)/shard_map/all_to_all | solution.py:45
  69.7 42.4 %all-to-all-start = ((bf16[16,24,1536]{2,1,0:T(8,128)(2,1)}), bf16[16,24,1536]{2,1,0:T(8,128)(2,1)}, u32[]{:S(2)}, u32[]{:S(2)}) async-start(bf16[16,24,1536]{2,1,0:T(8,128)(2,1)} %bitcast.4), calls=%async_computation | async-start | bytes 2359296 | tf_op jit(solution)/shard_map/all_to_all | solution.py:46
  115.8 2.2 copy-start.8
  118.0 4.1 copy-start.5
  118.0 48.1 %all-to-all-start.2 = ((bf16[16,24,1536]{2,1,0:T(8,128)(2,1)}), bf16[16,24,1536]{2,1,0:T(8,128)(2,1)S(1)}, u32[]{:S(2)}, u32[]{:S(2)}) async-start(bf16[16,24,1536]{2,1,0:T(8,128)(2,1)} %bitcast.178), calls=%async_computation.2 | async-start | bytes 2359296 | tf_op jit(solution)/shard_map/all_to_all | solution.py:71
  121.8 242.0 %reduce-scatter.15.cloned.1.call-start = ((), (), s32[]{:S(2)}) async-start(), calls=%async_computation.12 | async-start | bytes 6684672
  220.4 5.3 slice-start
  222.9 2.8 slice-start.1
  222.9 3.7 slice-start.2
  225.5 2.2 slice-start.3
  227.7 2.6 copy-start.2
  230.3 2.6 copy-start.3
  234.9 5.3 slice-start
  237.4 2.8 slice-start.1
  237.4 3.7 slice-start.2
  240.0 2.2 slice-start.3
  242.2 2.6 copy-start.2
  244.8 2.6 copy-start.3
  249.4 5.3 slice-start
  251.9 2.8 slice-start.1
  251.9 3.7 slice-start.2
  254.5 2.2 slice-start.3
  256.7 2.6 copy-start.2
  259.3 2.6 copy-start.3
  263.9 5.3 slice-start
  266.4 2.8 slice-start.1
  266.4 3.7 slice-start.2
  269.0 2.2 slice-start.3
  271.2 2.6 copy-start.2
  273.8 2.6 copy-start.3
  297.3 140.3 %reduce-scatter.13.cloned.1.call-start = ((), (), s32[]{:S(2)}) async-start(), calls=%async_computation.11 | async-start | bytes 6684672
  318.2 1.3 copy-start.7
  318.2 187.1 %reduce-scatter.11.cloned.1.call-start = ((), (), s32[]{:S(2)}) async-start(), calls=%async_computation.8 | async-start | bytes 2506752 | tf_op jit(solution)/shard_map/reduce_scatter | solution.py:80
  323.6 1.1 copy-start.9
  323.6 249.0 %reduce-scatter.9.cloned.1.call-start = ((), (), s32[]{:S(2)}) async-start(), calls=%async_computation.7 | async-start | bytes 2506752 | tf_op jit(solution)/shard_map/reduce_scatter | solution.py:77
  328.8 243.8 %copy-start.1 = (bf16[1,1536,768]{2,1,0:T(8,128)(2,1)S(1)}, bf16[1,1536,768]{2,1,0:T(8,128)(2,1)}, u32[]{:S(2)}) copy-start(bf16[1,1536,768]{2,1,0:T(8,128)(2,1)} %param.20) | copy-start | bytes 7077892
Sparse Core Ops, SparseCore 0:
  9.9 88.9 all-gather.6
  100.7 70.5 all-gather.4
  297.4 66.4 reduce-scatter.14
  366.3 71.2 reduce-scatter.12
  440.6 64.6 reduce-scatter.10
  508.3 64.3 reduce-scatter.8
where the time goes:
time: 588 us; the launch traced here: 580 us
  waiting for transfers between devices  361 us (61%)
  local copies, waits for them, and re-layouts  115 us (20%)
  matrix products  65 us (11%)
  starting transfers between devices  20.7 us (4%)
  between operations  14.8 us (3%)
    unnamed x8, waiting for transfers between devices  107 us
    reduce_scatter x1, waiting for transfers between devices, per_device(): lax.psum_scatter(first_term.astype(jnp.bfloat16), 'ctx', scatter_dimensio...  67.4 us
    unnamed x32, local copies, waits for them, and re-layouts  65.7 us
    reduce_scatter x1, waiting for transfers between devices, per_device(): lax.psum_scatter(second_term.astype(jnp.bfloat16), 'ctx', scatter_dimensi...  65.5 us
    all_to_all x1, waiting for transfers between devices, per_device(): lax.all_to_all(back_send, 'exp', split_axis=0, concat_axis=0, tiled=True)  43.5 us
    all_to_all x1, waiting for transfers between devices, per_device(): lax.all_to_all(sent_rows.reshape(shape), 'exp', split_axis=0, concat_axis...  42.6 us
    all_to_all x1, waiting for transfers between devices, per_device(): lax.all_to_all(sent_grads.reshape(shape), 'exp', split_axis=0, concat_axi...  34.6 us
    while x48, local copies, waits for them, and re-layouts  22.3 us
  transfers between devices with their start and end apart: 9, of which 7 were waited for; matrix products, arithmetic and copies ran while one was open for 13% of the time, Pallas kernels for 0%

commit v1 on v0

v1 whole, which is shorter than its diff:
```python
import functools

import jax
import jax.numpy as jnp
from jax import lax
from jax.experimental import pallas as pl
from jax.experimental.pallas import tpu as pltpu
from jax.sharding import PartitionSpec as P

HEAD_DIM = 128
MESH = pl.DeviceIdType.MESH
F32 = jnp.float32
BF16 = jnp.bfloat16


def dot_nn(a, b):
    return lax.dot_general(a, b, (((1,), (0,)), ((), ())), preferred_element_type=F32)


def dot_nt(a, b):
    return lax.dot_general(a, b, (((1,), (1,)), ((), ())), preferred_element_type=F32)


def dot_tn(a, b):
    return lax.dot_general(a, b, (((0,), (0,)), ((), ())), preferred_element_type=F32)


def kernel(
    nx, nexp, group,
    ids_ref, gates_ref, q_ref, k_ref, v_ref, att_ref, og_ref, w1_ref, w2_ref,
    qg_ref, kg_ref, vg_ref, w1g_ref, w2g_ref,
    att, og, w1, w2, code, gate_row, pick, slot_gate, wide,
    send_rows, send_grads, send_back, got_rows, got_grads, got_back,
    rows, grads, upper, act, upg,
    q_all, k_all, v_all, g_all, probs, sums, got_sums, inverse, delta,
    dq, dk, dv, dq_pair, dq_far, dk_far, dv_far,
    t1, t2, t1_pair, t2_pair, t1_x, t2_x, t1_z, t2_z, out1, out2,
    local_sem, out_sem, a2a_send, a2a_recv, kv_send, kv_recv, b_send, b_recv, small_send, small_recv,
    rx_send, rx_recv, rq_send, rq_recv, rz_send, rz_recv, w_send, w_recv, wx_send, wx_recv,
):
    tok, width = att.shape
    ff = act.shape[1]
    heads = width // HEAD_DIM
    cap = send_rows.shape[1]
    scale = HEAD_DIM ** (-0.5)
    me = lax.axis_index("exp")
    ctx = lax.axis_index("ctx")
    core = lax.rem(ctx, 2)
    my_x = lax.rem(ctx // 2, nx)
    zl = ctx // (2 * nx)
    b_me = zl * 2 + core

    def ctx_of(z, x, c):
        return (z * nx + x) * 2 + c

    def b_dev(b):
        return {"ctx": ctx_of(b // 2, my_x, lax.rem(b, 2))}

    def x_dev(x):
        return {"ctx": ctx_of(zl, x, core)}

    sib = {"ctx": ctx_of(zl, my_x, 1 - core)}
    zpart = {"ctx": ctx_of(1 - zl, my_x, core)}
    b_sib, b_z, b_diag = zl * 2 + 1 - core, (1 - zl) * 2 + core, (1 - zl) * 2 + 1 - core

    def remote(src, dst, ssem, rsem, dev):
        return pltpu.make_async_remote_copy(
            src_ref=src, dst_ref=dst, send_sem=ssem, recv_sem=rsem, device_id=dev, device_id_type=MESH
        )

    def blk(ref, i):
        return ref.at[pl.ds(pl.multiple_of(i * tok, tok), tok)]

    barrier = pltpu.get_barrier_semaphore()

    @pl.loop(1, nexp)
    def _(k):
        pl.semaphore_signal(barrier, inc=1, device_id={"exp": lax.rem(me + k, nexp)}, device_id_type=MESH)

    @pl.loop(1, nx)
    def _(k):
        pl.semaphore_signal(barrier, inc=1, device_id=x_dev(lax.rem(my_x + k, nx)), device_id_type=MESH)

    @pl.loop(1, 4)
    def _(k):
        pl.semaphore_signal(barrier, inc=1, device_id=b_dev(lax.rem(b_me + k, 4)), device_id_type=MESH)

    local = [
        pltpu.make_async_copy(s, d, local_sem.at[i])
        for i, (s, d) in enumerate(
            (
                (att_ref, att), (og_ref, og), (w1_ref, w1), (w2_ref, w2),
                (q_ref, blk(q_all, b_me)), (k_ref, blk(k_all, my_x)), (v_ref, blk(v_all, my_x)),
            )
        )
    ]
    for c in local:
        c.start()

    expert = lax.broadcasted_iota(jnp.int32, (nexp, tok), 0)
    first, second = ids_ref[0:1, :] == expert, ids_ref[1:2, :] == expert
    member = jnp.where(first | second, 1.0, 0.0)
    earlier = jnp.where(
        lax.broadcasted_iota(jnp.int32, (tok, tok), 0) < lax.broadcasted_iota(jnp.int32, (tok, tok), 1), 1.0, 0.0
    )
    before = dot_nn(member.astype(BF16), earlier.astype(BF16))
    code[...] = jnp.where(member > 0.5, before, -1.0)
    gate_row[...] = jnp.where(first, gates_ref[0:1, :], 0.0) + jnp.where(second, gates_ref[1:2, :], 0.0)
    slot = lax.broadcasted_iota(jnp.int32, (cap, tok), 0).astype(F32)

    @pl.loop(0, nexp)
    def _(e):
        at = pl.ds(pl.multiple_of(e * cap, 8), cap)
        here = jnp.broadcast_to(code[pl.ds(e, 1), :], (cap, tok)) == slot
        gate = jnp.broadcast_to(gate_row[pl.ds(e, 1), :], (cap, tok))
        wide[at, pl.ds(0, tok)] = jnp.where(here, 1.0, 0.0)
        slot_gate[at, :] = jnp.broadcast_to(
            jnp.sum(jnp.where(here, gate, 0.0), axis=1, keepdims=True), (cap, tok)
        )

    pick[...] = wide[:, pl.ds(0, tok)].astype(BF16)
    pl.semaphore_wait(barrier, nexp - 1 + nx - 1 + 3)

    def tiles(n, size):
        return pl.loop(0, n // size)

    def cols(j, size):
        return pl.ds(pl.multiple_of(j * size, 128), size)

    wide_tile = 256

    def dispatch(buffer, got, which):
        @pl.loop(1, nexp + 1)
        def _(k):
            e = lax.rem(me + k, nexp)
            buffer[e] = wide[pl.ds(pl.multiple_of(e * cap, 8), cap), :].astype(BF16)

            @pl.when(k < nexp)
            def _():
                remote(
                    buffer.at[e], got.at[me], a2a_send.at[which, e], a2a_recv.at[which, me], {"exp": e}
                ).start()

            @pl.when(k == nexp)
            def _():
                got[me] = buffer[me]

    def arrived(buffer, got, which):
        @pl.loop(1, nexp)
        def _(k):
            e = lax.rem(me + nexp - k, nexp)
            remote(
                buffer.at[e], got.at[e], a2a_send.at[which, e], a2a_recv.at[which, e], {"exp": e}
            ).wait_recv()

    def unpack(got, out):
        @pl.loop(0, nexp)
        def _(e):
            wide[pl.ds(pl.multiple_of(e * cap, 8), cap), :] = got[e].astype(F32)

        @tiles(width, wide_tile)
        def _(j):
            out[:, cols(j, wide_tile)] = wide[:, cols(j, wide_tile)].astype(BF16)

    local[0].wait()

    @tiles(width, wide_tile)
    def _(j):
        wide[:, cols(j, wide_tile)] = dot_nn(pick[...], att[:, cols(j, wide_tile)])

    dispatch(send_rows, got_rows, 0)
    local[1].wait()

    @tiles(width, wide_tile)
    def _(j):
        wide[:, cols(j, wide_tile)] = dot_nn(pick[...], og[:, cols(j, wide_tile)]) * slot_gate[:, 0:1]

    dispatch(send_grads, got_grads, 1)

    def b_start(src, buf, which):
        remote(src, blk(buf, b_me), b_send.at[which, 0], b_recv.at[which, 0], sib).start()
        remote(src, blk(buf, b_me), b_send.at[which, 1], b_recv.at[which, 1], zpart).start()

    def b_forward(buf, which):
        mine = blk(buf, b_z)
        remote(mine, mine, b_send.at[which, 1], b_recv.at[which, 1], zpart).wait_recv()
        remote(mine, mine, b_send.at[which, 2], b_recv.at[which, 2], sib).start()

    def b_finish(buf, which):
        s, d = blk(buf, b_sib), blk(buf, b_diag)
        remote(s, s, b_send.at[which, 0], b_recv.at[which, 0], sib).wait_recv()
        remote(d, d, b_send.at[which, 2], b_recv.at[which, 2], sib).wait_recv()

    b_start(q_ref, q_all, 0)
    for which, (src, buf) in enumerate(((k_ref, k_all), (v_ref, v_all))):
        for k in range(1, nx):
            remote(
                src, blk(buf, my_x), kv_send.at[which, k], kv_recv.at[which, k], x_dev(lax.rem(my_x + k, nx))
            ).start()

    def kv_wait(which, buf):
        for k in range(1, nx):
            x = lax.rem(my_x + nx - k, nx)
            remote(blk(buf, x), blk(buf, x), kv_send.at[which, k], kv_recv.at[which, k], x_dev(x)).wait_recv()

    b_forward(q_all, 0)
    local[4].wait()
    local[5].wait()
    local[6].wait()
    kv_wait(0, k_all)
    b_finish(q_all, 0)

    sums[...] = jnp.ones_like(sums)
    nkeys, nq = nx * tok, 4 * tok
    half = 2 * tok

    @pl.loop(0, heads)
    def _(h):
        c = cols(h, HEAD_DIM)
        qh = q_all[:, c]
        total = jnp.zeros((1, nq), F32)
        for i in range(nkeys // half):
            e = jnp.exp(dot_nt(k_all[pl.ds(i * half, half), c], qh) * scale)
            probs[h, pl.ds(i * half, half), :] = e.astype(BF16)
            total = total + jnp.sum(e, axis=0, keepdims=True)
        sums[pl.ds(h, 1), :] = total

    for k in range(1, 4):
        remote(
            sums, got_sums.at[b_me], small_send.at[0, k], small_recv.at[0, k], b_dev(lax.rem(b_me + k, 4))
        ).start()

    arrived(send_rows, got_rows, 0)
    unpack(got_rows, rows)
    local[2].wait()
    local[3].wait()
    t = min(256, ff)

    @tiles(ff, t)
    def _(j):
        upper[:, cols(j, t)] = dot_nn(rows[...], w1[:, cols(j, t)])

    arrived(send_grads, got_grads, 1)
    unpack(got_grads, grads)

    @tiles(ff, t)
    def _(j):
        u = upper[:, cols(j, t)]
        sig = jax.nn.sigmoid(u)
        act[:, cols(j, t)] = (u * sig).astype(BF16)
        back = dot_nt(grads[...], w2[cols(j, t), :])
        upg[:, cols(j, t)] = (back * sig * (1.0 + u * (1.0 - sig))).astype(BF16)

    @tiles(width, wide_tile)
    def _(j):
        wide[:, cols(j, wide_tile)] = dot_nt(upg[...], w1[cols(j, wide_tile), :])

    dispatch(send_back, got_back, 2)

    nblk = nx * 4
    wr1, wr2 = width // nblk, ff // nblk

    @pl.loop(0, 4)
    def _(j):
        term = dot_tn(rows[:, cols(j, width // 4)], upg[...]).astype(BF16)
        for i in range(nx):
            t1[i % 2, j * (nx // 2) + i // 2] = term[i * wr1 : (i + 1) * wr1]

    @pl.loop(0, 2)
    def _(j):
        term = dot_tn(act[:, cols(j, ff // 2)], grads[...]).astype(BF16)
        for i in range(2 * nx):
            t2[i % 2, j * nx + i // 2] = term[i * wr2 : (i + 1) * wr2]

    w_pair = (
        remote(t1.at[1 - core], t1_pair, w_send.at[0], w_recv.at[0], sib),
        remote(t2.at[1 - core], t2_pair, w_send.at[1], w_recv.at[1], sib),
    )
    for c in w_pair:
        c.start()
    for c in w_pair:
        c.wait()
    for i in range(2):

        @pl.loop(0, nx)
        def _(x):
            q = i * nx + x
            t1[1 - core, q] = (t1[core, q].astype(F32) + t1_pair[q].astype(F32)).astype(BF16)
            t2[1 - core, q] = (t2[core, q].astype(F32) + t2_pair[q].astype(F32)).astype(BF16)

    def w_x(k, i, to_x, dev):
        q = i * nx + to_x
        return (
            remote(t1.at[1 - core, q], t1_x.at[k, i], wx_send.at[0, k, i], wx_recv.at[0, k, i], dev),
            remote(t2.at[1 - core, q], t2_x.at[k, i], wx_send.at[1, k, i], wx_recv.at[1, k, i], dev),
        )

    for k in range(1, nx):
        x = lax.rem(my_x + k, nx)
        for i in range(2):
            for c in w_x(k, i, x, x_dev(x)):
                c.start()

    arrived(send_back, got_back, 2)
    unpack(got_back, rows)
    mine = pl.ds(pl.multiple_of(b_me * tok, tok), tok)
    ones = jnp.ones((8, HEAD_DIM), F32)

    @pl.loop(0, heads)
    def _(h):
        c = cols(h, HEAD_DIM)
        g = (og[:, c].astype(F32) + dot_tn(pick[...], rows[:, c])).astype(BF16)
        g_all[mine, c] = g
        d = lax.dot_general(
            ones, g.astype(F32) * att[:, c].astype(F32), (((1,), (1,)), ((), ())),
            preferred_element_type=F32, precision=lax.Precision.HIGHEST,
        )
        delta[b_me, pl.ds(h, 1), :] = d[0:1, :]

    b_start(blk(g_all, b_me), g_all, 1)

    def lanes(b):
        return delta.at[b]

    for k in range(1, 4):
        remote(
            lanes(b_me), lanes(b_me), small_send.at[1, k], small_recv.at[1, k], b_dev(lax.rem(b_me + k, 4))
        ).start()
    for k in range(1, 4):
        b = lax.rem(b_me + 4 - k, 4)
        remote(sums, got_sums.at[b], small_send.at[0, k], small_recv.at[0, k], b_dev(b)).wait_recv()
    got_sums[b_me] = sums[...]
    inverse[...] = 1.0 / (got_sums[0] + got_sums[1] + got_sums[2] + got_sums[3])
    kv_wait(1, v_all)
    b_forward(g_all, 1)
    for k in range(1, 4):
        b = lax.rem(b_me + 4 - k, 4)
        remote(lanes(b), lanes(b), small_send.at[1, k], small_recv.at[1, k], b_dev(b)).wait_recv()
    b_finish(g_all, 1)

    ngroup = heads // group
    gw = group * HEAD_DIM

    def part(ref, i, g):
        return ref.at[pl.ds(pl.multiple_of(i * tok, tok), tok), cols(g, gw)]

    def x_copies(g, k, to):
        return [
            remote(
                part(src, to, g), far.at[k - 1, :, cols(g, gw)], rx_send.at[w, k, g], rx_recv.at[w, k, g], x_dev(to)
            )
            for w, (src, far) in enumerate(((dk, dk_far), (dv, dv_far)))
        ]

    def pair_copies(g):
        return [
            remote(
                part(dq, i * 2 + 1 - core, g), dq_pair.at[i, :, cols(g, gw)], rq_send.at[i, g], rq_recv.at[i, g], sib
            )
            for i in range(2)
        ]

    def far_copy(g):
        return remote(part(dq, b_z, g), dq_far.at[:, cols(g, gw)], rz_send.at[g], rz_recv.at[g], zpart)

    def second_step(g):
        for c in pair_copies(g):
            c.wait_recv()
        rows_z = pl.ds(pl.multiple_of(b_z * tok, tok), tok)
        dq[rows_z, cols(g, gw)] = (
            dq[rows_z, cols(g, gw)].astype(F32) + dq_pair[1 - zl, :, cols(g, gw)].astype(F32)
        ).astype(BF16)
        far_copy(g).start()

    @pl.loop(0, ngroup)
    def _(g):
        @pl.loop(0, group)
        def _(i):
            h = g * group + i
            c = cols(h, HEAD_DIM)
            qh, gh = q_all[:, c], g_all[:, c]
            inv = inverse[pl.ds(h, 1), :]
            dl = jnp.concatenate([delta[b, pl.ds(h, 1), :] for b in range(4)], axis=1)
            q_acc = jnp.zeros((nq, HEAD_DIM), F32)
            for n in range(nkeys // half):
                r = pl.ds(n * half, half)
                kh = k_all[r, c]
                p = probs[h, r, :].astype(F32) * inv
                s = (p * (dot_nt(v_all[r, c], gh) - dl)).astype(BF16)
                dv[r, c] = dot_nn(p.astype(BF16), gh).astype(BF16)
                dk[r, c] = (dot_nn(s, qh) * scale).astype(BF16)
                q_acc = q_acc + dot_tn(s, kh)
            dq[:, c] = (q_acc * scale).astype(BF16)

        for c in pair_copies(g):
            c.start()
        for k in range(1, nx):
            for c in x_copies(g, k, lax.rem(my_x + k, nx)):
                c.start()

        @pl.when(g >= 1)
        def _():
            second_step(g - 1)

    second_step(ngroup - 1)

    for k in range(1, nx):
        for i in range(2):
            for c in w_x(k, i, my_x, x_dev(lax.rem(my_x + nx - k, nx))):
                c.wait_recv()
    for i in range(2):
        q = i * nx + my_x
        s1, s2 = t1[1 - core, q].astype(F32), t2[1 - core, q].astype(F32)
        for k in range(1, nx):
            s1, s2 = s1 + t1_x[k, i].astype(F32), s2 + t2_x[k, i].astype(F32)
        t1[core, i], t2[core, i] = s1.astype(BF16), s2.astype(BF16)
    w_z = (
        remote(t1.at[core, 1 - zl], t1_z, w_send.at[2], w_recv.at[2], zpart),
        remote(t2.at[core, 1 - zl], t2_z, w_send.at[3], w_recv.at[3], zpart),
    )
    for c in w_z:
        c.start()

    rows_x = pl.ds(pl.multiple_of(my_x * tok, tok), tok)

    @pl.loop(0, ngroup)
    def _(g):
        c = cols(g, gw)
        for k in range(1, nx):
            for d in x_copies(g, k, my_x):
                d.wait_recv()
        for src, far, out in ((dk, dk_far, 2), (dv, dv_far, 3)):
            total = src[rows_x, c].astype(F32)
            for k in range(1, nx):
                total = total + far[k - 1, :, c].astype(F32)
            src[rows_x, c] = total.astype(BF16)
        far_copy(g).wait_recv()
        dq[mine, c] = (
            dq[mine, c].astype(F32) + dq_pair[zl, :, c].astype(F32) + dq_far[:, c].astype(F32)
        ).astype(BF16)

    outs = [
        pltpu.make_async_copy(blk(dq, b_me), qg_ref, out_sem.at[0]),
        pltpu.make_async_copy(blk(dk, my_x), kg_ref, out_sem.at[1]),
        pltpu.make_async_copy(blk(dv, my_x), vg_ref, out_sem.at[2]),
    ]
    for c in outs:
        c.start()
    for c in w_z:
        c.wait()
    out1[...] = (t1[core, zl].astype(F32) + t1_z[...].astype(F32)).astype(BF16)
    out2[...] = (t2[core, zl].astype(F32) + t2_z[...].astype(F32)).astype(BF16)
    outs += [
        pltpu.make_async_copy(out1, w1g_ref, out_sem.at[3]),
        pltpu.make_async_copy(out2, w2g_ref, out_sem.at[4]),
    ]
    for c in outs[3:]:
        c.start()

    for which, buffer, got in ((0, send_rows, got_rows), (1, send_grads, got_grads), (2, send_back, got_back)):

        @pl.loop(1, nexp)
        def _(k):
            e = lax.rem(me + k, nexp)
            remote(
                buffer.at[e], got.at[me], a2a_send.at[which, e], a2a_recv.at[which, me], {"exp": e}
            ).wait_send()

    for which, src, buf in ((0, q_ref, q_all), (1, blk(g_all, b_me), g_all)):
        remote(src, blk(buf, b_me), b_send.at[which, 0], b_recv.at[which, 0], sib).wait_send()
        remote(src, blk(buf, b_me), b_send.at[which, 1], b_recv.at[which, 1], zpart).wait_send()
        z = blk(buf, b_z)
        remote(z, z, b_send.at[which, 2], b_recv.at[which, 2], sib).wait_send()
    for which, (src, buf) in enumerate(((k_ref, k_all), (v_ref, v_all))):
        for k in range(1, nx):
            remote(
                src, blk(buf, my_x), kv_send.at[which, k], kv_recv.at[which, k], x_dev(lax.rem(my_x + k, nx))
            ).wait_send()
    for k in range(1, 4):
        dev = b_dev(lax.rem(b_me + k, 4))
        remote(sums, got_sums.at[b_me], small_send.at[0, k], small_recv.at[0, k], dev).wait_send()
        remote(lanes(b_me), lanes(b_me), small_send.at[1, k], small_recv.at[1, k], dev).wait_send()
    for k in range(1, nx):
        x = lax.rem(my_x + k, nx)
        for i in range(2):
            for c in w_x(k, i, x, x_dev(x)):
                c.wait_send()

    @pl.loop(0, ngroup)
    def _(g):
        for c in pair_copies(g):
            c.wait_send()
        for k in range(1, nx):
            for c in x_copies(g, k, lax.rem(my_x + k, nx)):
                c.wait_send()
        far_copy(g).wait_send()

    for c in outs:
        c.wait()


def per_device(queries, key_states, value_states, attended, output_grad, expert_ids, gate_weights, w_in, w_out):
    tok, width = queries.shape[1:]
    ff = w_in.shape[2]
    heads = width // HEAD_DIM
    nexp, nctx = lax.axis_size("exp"), lax.axis_size("ctx")
    nx = nctx // 4
    cap = 3 * tok // nexp
    pairs = nexp * cap
    group = 3 if heads % 3 == 0 else 2
    ngroup = heads // group
    hp = -(-heads // 8) * 8
    wr1, wr2 = width // nctx, ff // nctx
    dma = pltpu.SemaphoreType.DMA
    v = pltpu.VMEM
    scratch = [
        v((tok, width), BF16), v((tok, width), BF16), v((width, ff), BF16), v((ff, width), BF16),
        v((nexp, tok), F32), v((nexp, tok), F32), v((pairs, tok), BF16), v((pairs, tok), F32), v((pairs, width), F32),
        *[v((nexp, cap, width), BF16) for _ in range(6)],
        v((pairs, width), BF16), v((pairs, width), BF16), v((pairs, ff), F32), v((pairs, ff), BF16), v((pairs, ff), BF16),
        v((4 * tok, width), BF16), v((nx * tok, width), BF16), v((nx * tok, width), BF16), v((4 * tok, width), BF16),
        v((heads, nx * tok, 4 * tok), BF16),
        v((hp, 4 * tok), F32), v((4, hp, 4 * tok), F32), v((hp, 4 * tok), F32), v((4, hp, tok), F32),
        v((4 * tok, width), BF16), v((nx * tok, width), BF16), v((nx * tok, width), BF16),
        v((2, tok, width), BF16), v((tok, width), BF16),
        v((nx - 1, tok, width), BF16), v((nx - 1, tok, width), BF16),
        v((2, 2 * nx, wr1, ff), BF16), v((2, 2 * nx, wr2, width), BF16),
        v((2 * nx, wr1, ff), BF16), v((2 * nx, wr2, width), BF16),
        v((nx, 2, wr1, ff), BF16), v((nx, 2, wr2, width), BF16),
        v((wr1, ff), BF16), v((wr2, width), BF16), v((wr1, ff), BF16), v((wr2, width), BF16),
        dma((7,)), dma((5,)), dma((3, nexp)), dma((3, nexp)), dma((2, nx)), dma((2, nx)), dma((2, 3)), dma((2, 3)),
        dma((2, 4)), dma((2, 4)), dma((2, nx, ngroup)), dma((2, nx, ngroup)), dma((2, ngroup)), dma((2, ngroup)),
        dma((ngroup,)), dma((ngroup,)), dma((4,)), dma((4,)), dma((2, nx, 2)), dma((2, nx, 2)),
    ]
    block = jax.ShapeDtypeStruct((tok, width), BF16)
    hbm = pl.BlockSpec(memory_space=pl.ANY)
    small = pl.BlockSpec(memory_space=pltpu.VMEM)
    qg, kg, vg, g1, g2 = pl.pallas_call(
        functools.partial(kernel, nx, nexp, group),
        out_shape=[
            block, block, block,
            jax.ShapeDtypeStruct((wr1, ff), BF16), jax.ShapeDtypeStruct((wr2, width), BF16),
        ],
        in_specs=[small] * 2 + [hbm] * 7,
        out_specs=[hbm] * 5,
        scratch_shapes=scratch,
        compiler_params=pltpu.CompilerParams(
            collective_id=0, has_side_effects=True, vmem_limit_bytes=60 * 1024 * 1024
        ),
        name="block_backward",
    )(
        expert_ids[0].T, gate_weights[0].T, queries[0], key_states[0], value_states[0], attended[0], output_grad[0],
        w_in[0], w_out[0],
    )
    return qg[None], kg[None], vg[None], g1[None], g2[None]


def solution(mesh):
    stream = P("exp", "ctx", None)
    return jax.shard_map(
        per_device,
        mesh=mesh,
        in_specs=(stream,) * 7 + (P("exp", None, None),) * 2,
        out_specs=(stream,) * 5,
        check_vma=False,
    )
```

time: 588 us -> 181 us (0.31)
  the two profiles are of different devices: /device:TPU:1 before, /device:TPU:121 now
where the time goes in v1:
time: 181 us
  Pallas kernels  174 us (96%)
  local copies, waits for them, and re-layouts  6.67 us (4%)
    pallas_call x1, Pallas kernels, per_device(): pl.pallas_call(functools.partial(kernel, nx, nexp, group), out_shape=[blo...  174 us
    unnamed x9, local copies, waits for them, and re-layouts  6.67 us

profile of v1, /device:TPU:121, one launch (start us, length us, event | category | flops | bytes accessed | tf_op | source)
XLA Modules:
  0.0 181.0 jit_solution(13576503387122625889)
XLA Ops:
  0.6 173.7 %block_backward.1 = (bf16[128,1536]{1,0:T(8,128)(2,1)}, bf16[128,1536]{1,0:T(8,128)(2,1)}, bf16[128,1536]{1,0:T(8,128)(2,1)}, bf16[96,768]{1,0:T(8,128)(2,1)}, bf16[48,1536]{1,0:T(8,128)(2,1)}) custom-call(s32[2,128]{1,0:T(2,128)} %bitcast.30, f32[2,128]{1,0:T(2,128)} %bitcast.31, bf16[128,1536]{1,0:T(8,128)(2,1)} %bitcast.20, bf16[128,1536]{1,0:T(8,128)(2,1)} %bitcast.21, ...), custom_call_target="tpu_custom_call" | custom-call | tf_op jit(solution)/shard_map/block_backward/pallas_call | solution.py:538
  174.3 0.0 copy-start.1
  174.3 0.0 copy-start
  174.3 1.8 %copy.19 = bf16[1,128,1536]{2,1,0:T(8,128)(2,1)} copy(bf16[1,128,1536]{2,1,0:T(8,128)(2,1)} %bitcast.27) | data formatting | bytes 786432
  176.1 1.8 copy.20
  177.9 1.8 copy.21
  179.7 0.0 copy-done.1
  179.7 0.7 copy.22
  180.3 0.0 copy-done
  180.3 0.7 copy.23
Async XLA Ops:
  174.3 5.4 %copy-start.1 = (bf16[96,768]{1,0:T(8,128)(2,1)S(1)}, bf16[96,768]{1,0:T(8,128)(2,1)}, u32[]{:S(2)}) copy-start(bf16[96,768]{1,0:T(8,128)(2,1)} %get-tuple-element.13) | copy-start | bytes 442372
  174.3 6.0 %copy-start = (bf16[48,1536]{1,0:T(8,128)(2,1)S(1)}, bf16[48,1536]{1,0:T(8,128)(2,1)}, u32[]{:S(2)}) copy-start(bf16[48,1536]{1,0:T(8,128)(2,1)} %get-tuple-element.14) | copy-start | bytes 442372

commit v2 on v1

v2 whole, which is shorter than its diff:
```python
import functools

import jax
import jax.numpy as jnp
from jax import lax
from jax.experimental import pallas as pl
from jax.experimental.pallas import tpu as pltpu
from jax.sharding import PartitionSpec as P

HEAD_DIM = 128
MESH = pl.DeviceIdType.MESH
F32 = jnp.float32
BF16 = jnp.bfloat16
LAG = 2


def dot_nn(a, b):
    return lax.dot_general(a, b, (((1,), (0,)), ((), ())), preferred_element_type=F32)


def dot_nt(a, b):
    return lax.dot_general(a, b, (((1,), (1,)), ((), ())), preferred_element_type=F32)


def dot_tn(a, b):
    return lax.dot_general(a, b, (((0,), (0,)), ((), ())), preferred_element_type=F32)


def kernel(
    nx, ny, nexp, group,
    ids_ref, gates_ref, q_ref, k_ref, v_ref, att_ref, og_ref, w1_ref, w2_ref,
    qg_ref, kg_ref, vg_ref, w1g_ref, w2g_ref,
    att, og, w1, w2, code, gate_row, pick, pick_t, slot_gate, wide,
    send_rows, send_grads, send_back, got_rows, got_grads, got_back,
    rows, grads, upper, act, upg, stage, back,
    q_all, k_all, v_all, g_all, probs, sums, got_sums, inverse, delta,
    dq, dk, dv, dq_pair, dq_far, dk_far, dv_far, dk_relay, dv_relay,
    t1, t2, t1_pair, t2_pair, t1_x, t2_x, t1_relay, t2_relay, t1_z, t2_z, out1, out2,
    local_sem, out_sem, a2a_send, a2a_recv, back_send, back_recv, kv_send, kv_recv, q_send, q_recv, g_send, g_recv,
    sum_send, sum_recv, delta_send, delta_recv,
    rx_send, rx_recv, rq_send, rq_recv, rz_send, rz_recv, w_send, w_recv, wx_send, wx_recv,
):
    tok, width = att.shape
    ff = act.shape[1]
    heads = width // HEAD_DIM
    cap = send_rows.shape[1]
    scale = HEAD_DIM ** (-0.5)
    nz = nexp // ny
    gw = group * HEAD_DIM
    ngroup = heads // group
    me = lax.axis_index("exp")
    ctx = lax.axis_index("ctx")
    my_y, my_zh = lax.rem(me, ny), me // ny
    core = lax.rem(ctx, 2)
    my_x = lax.rem(ctx // 2, nx)
    zl = ctx // (2 * nx)
    b_me = zl * 2 + core

    def ahead(p):
        return lax.rem(my_zh + lax.rem(p, nz), nz) * ny + lax.rem(my_y + p // nz, ny)

    def behind(p):
        return lax.rem(my_zh + nz - lax.rem(p, nz), nz) * ny + lax.rem(my_y + ny - p // nz, ny)

    def ctx_of(z, x, c):
        return (z * nx + x) * 2 + c

    def b_dev(b):
        return {"ctx": ctx_of(b // 2, my_x, lax.rem(b, 2))}

    def x_dev(x):
        return {"ctx": ctx_of(zl, x, core)}

    sib = {"ctx": ctx_of(zl, my_x, 1 - core)}
    zpart = {"ctx": ctx_of(1 - zl, my_x, core)}
    b_sib, b_z, b_diag = zl * 2 + 1 - core, (1 - zl) * 2 + core, (1 - zl) * 2 + 1 - core

    def remote(src, dst, ssem, rsem, dev):
        return pltpu.make_async_remote_copy(
            src_ref=src, dst_ref=dst, send_sem=ssem, recv_sem=rsem, device_id=dev, device_id_type=MESH
        )

    def blk(ref, i):
        return ref.at[pl.ds(pl.multiple_of(i * tok, tok), tok)]

    def cols(j, size):
        return pl.ds(pl.multiple_of(j * size, 128), size)

    def part(ref, i, g):
        return ref.at[pl.ds(pl.multiple_of(i * tok, tok), tok), cols(g, gw)]

    def slots(p):
        return pl.ds(pl.multiple_of(p * cap, 8), cap)

    barrier = pltpu.get_barrier_semaphore()

    @pl.loop(1, nexp)
    def _(k):
        pl.semaphore_signal(barrier, inc=1, device_id={"exp": ahead(k)}, device_id_type=MESH)

    @pl.loop(1, nx)
    def _(k):
        pl.semaphore_signal(barrier, inc=1, device_id=x_dev(lax.rem(my_x + k, nx)), device_id_type=MESH)

    @pl.loop(1, 4)
    def _(k):
        pl.semaphore_signal(barrier, inc=1, device_id=b_dev(lax.rem(b_me + k, 4)), device_id_type=MESH)

    local = [
        pltpu.make_async_copy(s, d, local_sem.at[i])
        for i, (s, d) in enumerate(
            (
                (att_ref, att), (og_ref, og), (w1_ref, w1), (w2_ref, w2),
                (q_ref, blk(q_all, b_me)), (k_ref, blk(k_all, my_x)), (v_ref, blk(v_all, my_x)),
            )
        )
    ]
    for c in local:
        c.start()

    pl.semaphore_wait(barrier, nexp - 1 + nx - 1 + 3)
    q_sends = [
        remote(q_ref, blk(q_all, b_me), q_send.at[i], q_recv.at[i], dev) for i, dev in enumerate((sib, zpart))
    ]
    for c in q_sends:
        c.start()

    def kv_copy(which, k):
        src, buf = ((k_ref, k_all), (v_ref, v_all))[which]
        return remote(
            src, blk(buf, my_x), kv_send.at[which, k], kv_recv.at[which, k], x_dev(lax.rem(my_x + k, nx))
        )

    for which in range(2):
        for k in range(1, nx):
            kv_copy(which, k).start()
    expert = lax.broadcasted_iota(jnp.int32, (nexp, tok), 0)
    first, second = ids_ref[0:1, :] == expert, ids_ref[1:2, :] == expert
    member = jnp.where(first | second, 1.0, 0.0)
    earlier = jnp.where(
        lax.broadcasted_iota(jnp.int32, (tok, tok), 0) < lax.broadcasted_iota(jnp.int32, (tok, tok), 1), 1.0, 0.0
    )
    before = dot_nn(member.astype(BF16), earlier.astype(BF16))
    code[...] = jnp.where(member > 0.5, before, -1.0)
    gate_row[...] = jnp.where(first, gates_ref[0:1, :], 0.0) + jnp.where(second, gates_ref[1:2, :], 0.0)
    slot = lax.broadcasted_iota(jnp.int32, (cap, tok), 0).astype(F32)

    @pl.loop(0, nexp)
    def _(p):
        e = ahead(p)
        here = jnp.broadcast_to(code[pl.ds(e, 1), :], (cap, tok)) == slot
        gate = jnp.broadcast_to(gate_row[pl.ds(e, 1), :], (cap, tok))
        wide[slots(p), pl.ds(0, tok)] = jnp.where(here, 1.0, 0.0)
        slot_gate[slots(p), :] = jnp.broadcast_to(
            jnp.sum(jnp.where(here, gate, 0.0), axis=1, keepdims=True), (cap, tok)
        )

    picked = wide[:, pl.ds(0, tok)]
    pick[...] = picked.astype(BF16)
    pick_t[...] = picked.T.astype(BF16)

    def tiles(n, size):
        return pl.loop(0, n // size)

    wide_tile = 256
    nhalf = nexp // 2
    hrows = nhalf * cap

    def a2a(which, p):
        buffer, got = ((send_rows, got_rows), (send_grads, got_grads))[which]
        return remote(
            buffer.at[p], got.at[p], a2a_send.at[which, p], a2a_recv.at[which, p], {"exp": ahead(p)}
        )

    def fill(which, half):
        r = pl.ds(half * hrows, hrows)
        source, buffer = ((att, send_rows), (og, send_grads))[which]

        @tiles(width, wide_tile)
        def _(j):
            value = dot_nn(pick[r, :], source[:, cols(j, wide_tile)])
            wide[r, cols(j, wide_tile)] = value if which == 0 else value * slot_gate[r, 0:1]

        @pl.loop(half * nhalf, (half + 1) * nhalf)
        def _(p):
            buffer[p] = wide[slots(p), :].astype(BF16)

    def send(which, half):
        @pl.loop(max(1, half * nhalf), (half + 1) * nhalf)
        def _(p):
            a2a(which, p).start()

    def arrived(which, half):
        @pl.loop(max(1, half * nhalf), (half + 1) * nhalf)
        def _(p):
            a2a(which, p).wait_recv()

    local[0].wait()
    fill(0, 0)
    send(0, 0)
    local[1].wait()
    fill(1, 0)
    send(1, 0)
    fill(0, 1)
    send(0, 1)
    fill(1, 1)
    send(1, 1)
    got_rows[0] = send_rows[0]
    got_grads[0] = send_grads[0]

    def kv_wait(which, buf):
        for k in range(1, nx):
            x = lax.rem(my_x + nx - k, nx)
            remote(blk(buf, x), blk(buf, x), kv_send.at[which, k], kv_recv.at[which, k], x_dev(x)).wait_recv()

    t = min(256, ff)
    def back_copy(g, p):
        return remote(
            send_back.at[g, p], got_back.at[g, p], back_send.at[g, p], back_recv.at[g, p], {"exp": behind(p)}
        )

    def expert_half(half):
        r = pl.ds(half * hrows, hrows)

        def unpack(got, out):
            @pl.loop(half * nhalf, (half + 1) * nhalf)
            def _(p):
                wide[slots(p), :] = got[p].astype(F32)

            @tiles(width, wide_tile)
            def _(j):
                out[r, cols(j, wide_tile)] = wide[r, cols(j, wide_tile)].astype(BF16)

        arrived(0, half)
        unpack(got_rows, rows)
        if half == 0:
            local[2].wait()
            local[3].wait()

        @tiles(ff, t)
        def _(j):
            upper[:, cols(j, t)] = dot_nn(rows[r, :], w1[:, cols(j, t)])

        arrived(1, half)
        unpack(got_grads, grads)

        @tiles(ff, t)
        def _(j):
            u = upper[:, cols(j, t)]
            sig = jax.nn.sigmoid(u)
            act[r, cols(j, t)] = (u * sig).astype(BF16)
            d = dot_nt(grads[r, :], w2[cols(j, t), :])
            upg[r, cols(j, t)] = (d * sig * (1.0 + u * (1.0 - sig))).astype(BF16)

    expert_half(0)

    def q_forward():
        mine = blk(q_all, b_z)
        return remote(mine, mine, q_send.at[2], q_recv.at[2], sib)

    z, s, d = blk(q_all, b_z), blk(q_all, b_sib), blk(q_all, b_diag)
    remote(z, z, q_send.at[1], q_recv.at[1], zpart).wait_recv()
    q_forward().start()
    local[4].wait()
    local[5].wait()
    local[6].wait()
    kv_wait(0, k_all)
    remote(s, s, q_send.at[0], q_recv.at[0], sib).wait_recv()
    remote(d, d, q_send.at[2], q_recv.at[2], sib).wait_recv()
    sums[...] = jnp.ones_like(sums)
    nkeys, nq = nx * tok, 4 * tok
    part_keys = 2 * tok

    @pl.loop(0, heads)
    def _(h):
        c = cols(h, HEAD_DIM)
        qh = q_all[:, c]
        total = jnp.zeros((1, nq), F32)
        for i in range(nkeys // part_keys):
            e = jnp.exp(dot_nt(k_all[pl.ds(i * part_keys, part_keys), c], qh) * scale)
            probs[h, pl.ds(i * part_keys, part_keys), :] = e.astype(BF16)
            total = total + jnp.sum(e, axis=0, keepdims=True)
        sums[pl.ds(h, 1), :] = total

    def sum_copy(k):
        return remote(
            sums, got_sums.at[b_me], sum_send.at[k], sum_recv.at[k], b_dev(lax.rem(b_me + k, 4))
        )

    for k in range(1, 4):
        sum_copy(k).start()

    expert_half(1)

    @pl.loop(0, ngroup)
    def _(g):
        stage[...] = dot_nt(upg[...], w1[cols(g, gw), :])

        @pl.loop(0, nexp)
        def _(p):
            send_back[g, p] = stage[slots(p), :].astype(BF16)

        @pl.loop(1, nexp)
        def _(p):
            back_copy(g, p).start()

    nblk = nx * 4
    wr1, wr2 = width // nblk, ff // nblk
    x_next, x_far, x_prev = (lax.rem(my_x + k, nx) for k in range(1, 4))
    w_pair = (
        remote(t1.at[1 - core], t1_pair, w_send.at[0], w_recv.at[0], sib),
        remote(t2.at[1 - core], t2_pair, w_send.at[1], w_recv.at[1], sib),
    )

    @pl.loop(0, 4)
    def _(j):
        term = dot_tn(rows[:, cols(j, width // 4)], upg[...]).astype(BF16)
        for i in range(nx):
            t1[i % 2, j * (nx // 2) + i // 2] = term[i * wr1 : (i + 1) * wr1]

    w_pair[0].start()

    @pl.loop(0, 2)
    def _(j):
        term = dot_tn(act[:, cols(j, ff // 2)], grads[...]).astype(BF16)
        for i in range(2 * nx):
            t2[i % 2, j * nx + i // 2] = term[i * wr2 : (i + 1) * wr2]

    w_pair[1].start()

    def w_first(w):
        t, land, relay = ((t1, t1_x, t1_relay), (t2, t2_x, t2_relay))[w]
        return [
            remote(t.at[1 - core, i * nx + to], dst, wx_send.at[w, n], wx_recv.at[w, n], x_dev(dev))
            for n, (i, to, dst, dev) in enumerate(
                (
                    (0, x_far, relay.at[0], x_next), (1, x_far, relay.at[1], x_prev),
                    (1, x_next, land.at[0, 1], x_next), (0, x_prev, land.at[1, 0], x_prev),
                )
            )
        ]

    def w_second(w):
        t, land = ((t1, t1_x), (t2, t2_x))[w]
        return [
            remote(t.at[1 - core, i * nx + to], land.at[n, i], wx_send.at[w, 4 + n], wx_recv.at[w, 4 + n], x_dev(to))
            for n, (i, to) in enumerate(((0, x_next), (1, x_prev)))
        ]

    for w, (t, pair) in enumerate(((t1, t1_pair), (t2, t2_pair))):
        w_pair[w].wait()

        @pl.loop(0, 2 * nx)
        def _(q):
            t[1 - core, q] = (t[core, q].astype(F32) + pair[q].astype(F32)).astype(BF16)

        for c in w_first(w):
            c.start()

    def w_relay():
        for w, (t, relay) in enumerate(((t1, t1_relay), (t2, t2_relay))):
            for n, c in enumerate(w_first(w)[:2]):
                c.wait_recv()
                q = n * nx + (x_next, x_prev)[n]
                t[1 - core, q] = (t[1 - core, q].astype(F32) + relay[n].astype(F32)).astype(BF16)
                w_second(w)[n].start()

    w_z = (
        remote(t1.at[core, 1 - zl], t1_z, w_send.at[2], w_recv.at[2], zpart),
        remote(t2.at[core, 1 - zl], t2_z, w_send.at[3], w_recv.at[3], zpart),
    )

    def w_over_z():
        for w, (t, land) in enumerate(((t1, t1_x), (t2, t2_x))):
            for c in w_first(w)[2:] + w_second(w):
                c.wait_recv()
            for i in range(2):
                total = t[1 - core, i * nx + my_x].astype(F32) + land[0, i].astype(F32) + land[1, i].astype(F32)
                t[core, i] = total.astype(BF16)
            w_z[w].start()

    for k in range(1, 4):
        b = lax.rem(b_me + 4 - k, 4)
        remote(sums, got_sums.at[b], sum_send.at[k], sum_recv.at[k], b_dev(b)).wait_recv()
    got_sums[b_me] = sums[...]
    inverse[...] = 1.0 / (got_sums[0] + got_sums[1] + got_sums[2] + got_sums[3])
    kv_wait(1, v_all)

    mine = pl.ds(pl.multiple_of(b_me * tok, tok), tok)
    ones = jnp.ones((8, HEAD_DIM), F32)

    def g_sends(g):
        m = part(g_all, b_me, g)
        return [remote(m, m, g_send.at[i, g], g_recv.at[i, g], dev) for i, dev in enumerate((sib, zpart))]

    def g_forward(g):
        m = part(g_all, b_z, g)
        return remote(m, m, g_send.at[2, g], g_recv.at[2, g], sib)

    def delta_copy(g, k):
        m = delta.at[g, b_me]
        return remote(m, m, delta_send.at[g, k], delta_recv.at[g, k], b_dev(lax.rem(b_me + k, 4)))

    def combine(g):
        @pl.loop(1, nexp)
        def _(p):
            back_copy(g, p).wait_recv()

        stage[slots(0), :] = send_back[g, 0].astype(F32)

        @pl.loop(1, nexp)
        def _(p):
            stage[slots(p), :] = got_back[g, p].astype(F32)

        back[...] = stage[...].astype(BF16)
        c = cols(g, gw)
        total = (og[:, c].astype(F32) + dot_nn(pick_t[...], back[...])).astype(BF16)
        g_all[mine, c] = total
        for d in g_sends(g):
            d.start()
        prod = total.astype(F32) * att[:, c].astype(F32)
        for i in range(group):
            d = lax.dot_general(
                ones, prod[:, i * HEAD_DIM : (i + 1) * HEAD_DIM], (((1,), (1,)), ((), ())),
                preferred_element_type=F32, precision=lax.Precision.HIGHEST,
            )
            delta[g, b_me, i : i + 1, :] = d[0:1, :]
        for k in range(1, 4):
            delta_copy(g, k).start()

    def forward(g):
        m = part(g_all, b_z, g)
        remote(m, m, g_send.at[1, g], g_recv.at[1, g], zpart).wait_recv()
        g_forward(g).start()

    def gathered(g):
        for k in range(1, 4):
            b = lax.rem(b_me + 4 - k, 4)
            m = delta.at[g, b]
            remote(m, m, delta_send.at[g, k], delta_recv.at[g, k], b_dev(b)).wait_recv()
        m = part(g_all, b_sib, g)
        remote(m, m, g_send.at[0, g], g_recv.at[0, g], sib).wait_recv()
        m = part(g_all, b_diag, g)
        remote(m, m, g_send.at[2, g], g_recv.at[2, g], sib).wait_recv()

    half_block = tok // 2

    def half_part(ref, i, n, g):
        return ref.at[pl.ds(pl.multiple_of(i * tok + n * half_block, half_block), half_block), cols(g, gw)]

    def half_of(ref, k, n, g):
        return ref.at[k, pl.ds(n * half_block, half_block), cols(g, gw)]

    kv_parts = ((dk, dk_far, dk_relay), (dv, dv_far, dv_relay))

    def x_first(w, g):
        src, far, relay = kv_parts[w]
        return [
            remote(half_part(src, to, i, g), dst, rx_send.at[w, n, g], rx_recv.at[w, n, g], x_dev(dev))
            for n, (i, to, dst, dev) in enumerate(
                (
                    (0, x_far, relay.at[0, :, cols(g, gw)], x_next), (1, x_far, relay.at[1, :, cols(g, gw)], x_prev),
                    (1, x_next, half_of(far, 0, 1, g), x_next), (0, x_prev, half_of(far, 1, 0, g), x_prev),
                )
            )
        ]

    def x_second(w, g):
        src, far, _ = kv_parts[w]
        return [
            remote(
                half_part(src, to, n, g), half_of(far, n, n, g), rx_send.at[w, 4 + n, g], rx_recv.at[w, 4 + n, g], x_dev(to)
            )
            for n, to in enumerate((x_next, x_prev))
        ]

    def x_relay(g):
        for w, (src, _, relay) in enumerate(kv_parts):
            for n, c in enumerate(x_first(w, g)[:2]):
                c.wait_recv()
                r = pl.ds(pl.multiple_of((x_next, x_prev)[n] * tok + n * half_block, half_block), half_block)
                k = cols(g, gw)
                src[r, k] = (src[r, k].astype(F32) + relay[n, :, k].astype(F32)).astype(BF16)
                x_second(w, g)[n].start()

    def pair_copies(g):
        return [
            remote(
                part(dq, i * 2 + 1 - core, g), dq_pair.at[i, :, cols(g, gw)], rq_send.at[i, g], rq_recv.at[i, g], sib
            )
            for i in range(2)
        ]

    def far_copy(g):
        return remote(part(dq, b_z, g), dq_far.at[:, cols(g, gw)], rz_send.at[g], rz_recv.at[g], zpart)

    def attention(g):
        gathered(g)

        @pl.loop(0, group)
        def _(i):
            h = g * group + i
            c = cols(h, HEAD_DIM)
            qh, gh = q_all[:, c], g_all[:, c]
            inv = inverse[pl.ds(h, 1), :]
            dl = jnp.concatenate([delta[g, b, pl.ds(i, 1), :] for b in range(4)], axis=1)
            q_acc = jnp.zeros((nq, HEAD_DIM), F32)
            for n in range(nkeys // part_keys):
                r = pl.ds(n * part_keys, part_keys)
                kh = k_all[r, c]
                p = probs[h, r, :].astype(F32) * inv
                s = (p * (dot_nt(v_all[r, c], gh) - dl)).astype(BF16)
                dv[r, c] = dot_nn(p.astype(BF16), gh).astype(BF16)
                dk[r, c] = (dot_nn(s, qh) * scale).astype(BF16)
                q_acc = q_acc + dot_tn(s, kh)
            dq[:, c] = (q_acc * scale).astype(BF16)

        for w in range(2):
            for c in x_first(w, g):
                c.start()
        for c in pair_copies(g):
            c.start()

    def second_step(g):
        for c in pair_copies(g):
            c.wait_recv()
        rows_z = pl.ds(pl.multiple_of(b_z * tok, tok), tok)
        dq[rows_z, cols(g, gw)] = (
            dq[rows_z, cols(g, gw)].astype(F32) + dq_pair[1 - zl, :, cols(g, gw)].astype(F32)
        ).astype(BF16)
        far_copy(g).start()

    @pl.loop(0, ngroup + LAG)
    def _(step):
        @pl.when((step >= 1) & (step <= ngroup))
        def _():
            forward(step - 1)

        @pl.when(step < ngroup)
        def _():
            combine(step)

        @pl.when((step >= 1) & (step <= ngroup))
        def _():
            attention(step - 1)

        @pl.when((step >= 2) & (step < ngroup + 2))
        def _():
            second_step(step - 2)

        @pl.when(step == 1)
        def _():
            w_relay()

        @pl.when(step >= LAG)
        def _():
            x_relay(step - LAG)

        @pl.when(step == ngroup)
        def _():
            w_over_z()

    rows_x = pl.ds(pl.multiple_of(my_x * tok, tok), tok)

    @pl.loop(0, ngroup)
    def _(g):
        c = cols(g, gw)
        far_copy(g).wait_recv()
        dq[mine, c] = (
            dq[mine, c].astype(F32) + dq_pair[zl, :, c].astype(F32) + dq_far[:, c].astype(F32)
        ).astype(BF16)
        for w, (src, far, _) in enumerate(kv_parts):
            for d in x_first(w, g)[2:] + x_second(w, g):
                d.wait_recv()
            src[rows_x, c] = (
                src[rows_x, c].astype(F32) + far[0, :, c].astype(F32) + far[1, :, c].astype(F32)
            ).astype(BF16)

    outs = [
        pltpu.make_async_copy(blk(dq, b_me), qg_ref, out_sem.at[0]),
        pltpu.make_async_copy(blk(dk, my_x), kg_ref, out_sem.at[1]),
        pltpu.make_async_copy(blk(dv, my_x), vg_ref, out_sem.at[2]),
    ]
    for c in outs:
        c.start()
    for c in w_z:
        c.wait()
    out1[...] = (t1[core, zl].astype(F32) + t1_z[...].astype(F32)).astype(BF16)
    out2[...] = (t2[core, zl].astype(F32) + t2_z[...].astype(F32)).astype(BF16)
    outs += [
        pltpu.make_async_copy(out1, w1g_ref, out_sem.at[3]),
        pltpu.make_async_copy(out2, w2g_ref, out_sem.at[4]),
    ]
    for c in outs[3:]:
        c.start()

    @pl.loop(1, nexp)
    def _(p):
        a2a(0, p).wait_send()
        a2a(1, p).wait_send()

        @pl.loop(0, ngroup)
        def _(g):
            back_copy(g, p).wait_send()

    for c in q_sends:
        c.wait_send()
    q_forward().wait_send()
    for which in range(2):
        for k in range(1, nx):
            kv_copy(which, k).wait_send()
    for k in range(1, 4):
        sum_copy(k).wait_send()
    for w in range(2):
        for c in w_first(w) + w_second(w):
            c.wait_send()

    @pl.loop(0, ngroup)
    def _(g):
        for c in g_sends(g):
            c.wait_send()
        g_forward(g).wait_send()
        for k in range(1, 4):
            delta_copy(g, k).wait_send()
        for c in pair_copies(g):
            c.wait_send()
        for w in range(2):
            for c in x_first(w, g) + x_second(w, g):
                c.wait_send()
        far_copy(g).wait_send()

    for c in outs:
        c.wait()


def hand_out(*refs):
    n = len(refs) // 2
    for i in range(n):
        refs[n + i][...] = refs[i][...]


def per_device(queries, key_states, value_states, attended, output_grad, expert_ids, gate_weights, w_in, w_out):
    tok, width = queries.shape[1:]
    ff = w_in.shape[2]
    heads = width // HEAD_DIM
    nexp, nctx = lax.axis_size("exp"), lax.axis_size("ctx")
    nx, ny = nctx // 4, min(4, max(2, nexp // 4))
    cap = 3 * tok // nexp
    pairs = nexp * cap
    group = 3 if heads % 3 == 0 else 2
    ngroup, gw = heads // group, group * HEAD_DIM
    hp = -(-heads // 8) * 8
    wr1, wr2 = width // nctx, ff // nctx
    dma = pltpu.SemaphoreType.DMA
    v = pltpu.VMEM
    scratch = [
        v((tok, width), BF16), v((tok, width), BF16), v((width, ff), BF16), v((ff, width), BF16),
        v((nexp, tok), F32), v((nexp, tok), F32), v((pairs, tok), BF16), v((tok, pairs), BF16),
        v((pairs, tok), F32), v((pairs, width), F32),
        v((nexp, cap, width), BF16), v((nexp, cap, width), BF16), v((ngroup, nexp, cap, gw), BF16),
        v((nexp, cap, width), BF16), v((nexp, cap, width), BF16), v((ngroup, nexp, cap, gw), BF16),
        v((pairs, width), BF16), v((pairs, width), BF16), v((pairs // 2, ff), F32), v((pairs, ff), BF16), v((pairs, ff), BF16),
        v((pairs, gw), F32), v((pairs, gw), BF16),
        v((4 * tok, width), BF16), v((nx * tok, width), BF16), v((nx * tok, width), BF16), v((4 * tok, width), BF16),
        v((heads, nx * tok, 4 * tok), BF16),
        v((hp, 4 * tok), F32), v((4, hp, 4 * tok), F32), v((hp, 4 * tok), F32), v((ngroup, 4, 8, tok), F32),
        v((4 * tok, width), BF16), v((nx * tok, width), BF16), v((nx * tok, width), BF16),
        v((2, tok, width), BF16), v((tok, width), BF16),
        v((2, tok, width), BF16), v((2, tok, width), BF16),
        v((2, tok // 2, width), BF16), v((2, tok // 2, width), BF16),
        v((2, 2 * nx, wr1, ff), BF16), v((2, 2 * nx, wr2, width), BF16),
        v((2 * nx, wr1, ff), BF16), v((2 * nx, wr2, width), BF16),
        v((2, 2, wr1, ff), BF16), v((2, 2, wr2, width), BF16), v((2, wr1, ff), BF16), v((2, wr2, width), BF16),
        v((wr1, ff), BF16), v((wr2, width), BF16), v((wr1, ff), BF16), v((wr2, width), BF16),
        dma((7,)), dma((5,)), dma((2, nexp)), dma((2, nexp)), dma((ngroup, nexp)), dma((ngroup, nexp)), dma((2, nx)), dma((2, nx)),
        dma((3,)), dma((3,)), dma((3, ngroup)), dma((3, ngroup)), dma((4,)), dma((4,)), dma((ngroup, 4)), dma((ngroup, 4)),
        dma((2, 6, ngroup)), dma((2, 6, ngroup)), dma((2, ngroup)), dma((2, ngroup)),
        dma((ngroup,)), dma((ngroup,)), dma((4,)), dma((4,)), dma((2, 6)), dma((2, 6)),
    ]
    block = jax.ShapeDtypeStruct((tok, width), BF16)
    shapes = [block, block, block, jax.ShapeDtypeStruct((wr1, ff), BF16), jax.ShapeDtypeStruct((wr2, width), BF16)]
    hbm = pl.BlockSpec(memory_space=pl.ANY)
    small = pl.BlockSpec(memory_space=pltpu.VMEM)
    results = pl.pallas_call(
        functools.partial(kernel, nx, ny, nexp, group),
        out_shape=shapes,
        in_specs=[small] * 2 + [hbm] * 7,
        out_specs=[hbm] * 5,
        scratch_shapes=scratch,
        compiler_params=pltpu.CompilerParams(
            collective_id=0, has_side_effects=True, vmem_limit_bytes=60 * 1024 * 1024
        ),
        name="block_backward",
    )(
        expert_ids[0].T, gate_weights[0].T, queries[0], key_states[0], value_states[0], attended[0], output_grad[0],
        w_in[0], w_out[0],
    )
    results = pl.pallas_call(
        hand_out, out_shape=shapes, in_specs=[small] * 5, out_specs=[small] * 5, name="hand_out"
    )(*results)
    return tuple(r[None] for r in results)


def solution(mesh):
    stream = P("exp", "ctx", None)
    return jax.shard_map(
        per_device,
        mesh=mesh,
        in_specs=(stream,) * 7 + (P("exp", None, None),) * 2,
        out_specs=(stream,) * 5,
        check_vma=False,
    )
```

time: 181 us -> 151 us (0.83)
  the two profiles are of different devices: /device:TPU:121 before, /device:TPU:1 now
where the time goes in v2:
time: 151 us
  Pallas kernels  150 us (99%)
    pallas_call x1, Pallas kernels, per_device(): pl.pallas_call(functools.partial(kernel, nx, ny, nexp, group), out_shape=...  147 us

profile of v2, /device:TPU:1, one launch (start us, length us, event | category | flops | bytes accessed | tf_op | source)
XLA Modules:
  0.0 150.6 jit_solution(5969269227115811385)
XLA Ops:
  0.6 147.4 %block_backward.1 = (bf16[128,1536]{1,0:T(8,128)(2,1)}, bf16[128,1536]{1,0:T(8,128)(2,1)}, bf16[128,1536]{1,0:T(8,128)(2,1)}, bf16[96,768]{1,0:T(8,128)(2,1)}, bf16[48,1536]{1,0:T(8,128)(2,1)}) custom-call(s32[2,128]{1,0:T(2,128)} %bitcast.25, f32[2,128]{1,0:T(2,128)} %bitcast.26, bf16[128,1536]{1,0:T(8,128)(2,1)} %bitcast.20, bf16[128,1536]{1,0:T(8,128)(2,1)} %bitcast.21, ...), custom_call_target="tpu_custom_call" | custom-call | tf_op jit(solution)/shard_map/block_backward/pallas_call | solution.py:684
  148.1 2.5 %hand_out.1 = (bf16[128,1536]{1,0:T(8,128)(2,1)}, bf16[128,1536]{1,0:T(8,128)(2,1)}, bf16[128,1536]{1,0:T(8,128)(2,1)}, bf16[96,768]{1,0:T(8,128)(2,1)}, bf16[48,1536]{1,0:T(8,128)(2,1)}) custom-call(bf16[128,1536]{1,0:T(8,128)(2,1)} %get-tuple-element.15.refs_0_, bf16[128,1536]{1,0:T(8,128)(2,1)} %get-tuple-element.16.refs_1_, ...), custom_call_target="tpu_custom_call" | custom-call | tf_op jit(solution)/shard_map/hand_out/pallas_call | solution.py:698

commit v3 on v2

--- a/solution.py
+++ b/solution.py
@@ -12,6 +12,7 @@
 F32 = jnp.float32
 BF16 = jnp.bfloat16
 LAG = 2
+AHEAD = 2
 
 
 def dot_nn(a, b):
@@ -56,11 +57,29 @@
     zl = ctx // (2 * nx)
     b_me = zl * 2 + core
 
-    def ahead(p):
-        return lax.rem(my_zh + lax.rem(p, nz), nz) * ny + lax.rem(my_y + p // nz, ny)
-
-    def behind(p):
-        return lax.rem(my_zh + nz - lax.rem(p, nz), nz) * ny + lax.rem(my_y + ny - p // nz, ny)
+    place = ((zl, 0), (0, 1 + zl), (1 - zl, 3), (1, 1 + zl))
+    origin = ((0, zl), (1 + 2 * zl, 0), (1 + 2 * zl, 1), (2, 1 - zl))
+
+    def owner(dy, s):
+        return lax.rem(my_zh + s, nz) * ny + lax.rem(my_y + dy, ny)
+
+    def worker(dy, s):
+        return {"exp": owner(dy, s), "ctx": ctx_of(place[s][0], my_x, core)}
+
+    def source(dy, r):
+        s, z = origin[r]
+        return {
+            "exp": lax.rem(my_zh + nz - s, nz) * ny + lax.rem(my_y + ny - dy, ny), "ctx": ctx_of(z, my_x, core)
+        }
+
+    def chunks(first, last, body):
+        @pl.loop(first, last)
+        def _(dy):
+            for n in range(nz):
+                if n == 0:
+                    pl.when(dy > 0)(functools.partial(body, dy, n))
+                else:
+                    body(dy, n)
 
     def ctx_of(z, x, c):
         return (z * nx + x) * 2 + c
@@ -94,9 +113,11 @@
 
     barrier = pltpu.get_barrier_semaphore()
 
-    @pl.loop(1, nexp)
-    def _(k):
-        pl.semaphore_signal(barrier, inc=1, device_id={"exp": ahead(k)}, device_id_type=MESH)
+    def greet(dy, n):
+        for dev in (worker(dy, n), source(dy, n)):
+            pl.semaphore_signal(barrier, inc=1, device_id=dev, device_id_type=MESH)
+
+    chunks(0, ny, greet)
 
     @pl.loop(1, nx)
     def _(k):
@@ -118,7 +139,7 @@
     for c in local:
         c.start()
 
-    pl.semaphore_wait(barrier, nexp - 1 + nx - 1 + 3)
+    pl.semaphore_wait(barrier, 2 * (nexp - 1) + nx - 1 + 3)
     q_sends = [
         remote(q_ref, blk(q_all, b_me), q_send.at[i], q_recv.at[i], dev) for i, dev in enumerate((sib, zpart))
     ]
@@ -131,9 +152,8 @@
             src, blk(buf, my_x), kv_send.at[which, k], kv_recv.at[which, k], x_dev(lax.rem(my_x + k, nx))
         )
 
-    for which in range(2):
-        for k in range(1, nx):
-            kv_copy(which, k).start()
+    for k in range(1, nx):
+        kv_copy(0, k).start()
     expert = lax.broadcasted_iota(jnp.int32, (nexp, tok), 0)
     first, second = ids_ref[0:1, :] == expert, ids_ref[1:2, :] == expert
     member = jnp.where(first | second, 1.0, 0.0)
@@ -147,7 +167,7 @@
 
     @pl.loop(0, nexp)
     def _(p):
-        e = ahead(p)
+        e = owner(p // nz, lax.rem(p, nz))
         here = jnp.broadcast_to(code[pl.ds(e, 1), :], (cap, tok)) == slot
         gate = jnp.broadcast_to(gate_row[pl.ds(e, 1), :], (cap, tok))
         wide[slots(p), pl.ds(0, tok)] = jnp.where(here, 1.0, 0.0)
@@ -166,10 +186,13 @@
     nhalf = nexp // 2
     hrows = nhalf * cap
 
-    def a2a(which, p):
+    hy = ny // 2
+
+    def a2a(which, dy, s):
         buffer, got = ((send_rows, got_rows), (send_grads, got_grads))[which]
+        here, there = dy * nz + s, dy * nz + place[s][1]
         return remote(
-            buffer.at[p], got.at[p], a2a_send.at[which, p], a2a_recv.at[which, p], {"exp": ahead(p)}
+            buffer.at[here], got.at[there], a2a_send.at[which, here], a2a_recv.at[which, there], worker(dy, s)
         )
 
     def fill(which, half):
@@ -186,14 +209,16 @@
             buffer[p] = wide[slots(p), :].astype(BF16)
 
     def send(which, half):
-        @pl.loop(max(1, half * nhalf), (half + 1) * nhalf)
-        def _(p):
-            a2a(which, p).start()
+        chunks(half * hy, (half + 1) * hy, lambda dy, s: a2a(which, dy, s).start())
 
     def arrived(which, half):
-        @pl.loop(max(1, half * nhalf), (half + 1) * nhalf)
-        def _(p):
-            a2a(which, p).wait_recv()
+        buffer, got = ((send_rows, got_rows), (send_grads, got_grads))[which]
+
+        def wait(dy, r):
+            p = dy * nz + r
+            remote(buffer.at[p], got.at[p], a2a_send.at[which, p], a2a_recv.at[which, p], source(dy, r)).wait_recv()
+
+        chunks(half * hy, (half + 1) * hy, wait)
 
     local[0].wait()
     fill(0, 0)
@@ -205,6 +230,8 @@
     send(0, 1)
     fill(1, 1)
     send(1, 1)
+    for k in range(1, nx):
+        kv_copy(1, k).start()
     got_rows[0] = send_rows[0]
     got_grads[0] = send_grads[0]
 
@@ -214,10 +241,17 @@
             remote(blk(buf, x), blk(buf, x), kv_send.at[which, k], kv_recv.at[which, k], x_dev(x)).wait_recv()
 
     t = min(256, ff)
-    def back_copy(g, p):
+    def back_copy(g, dy, r):
+        here, there = dy * nz + r, dy * nz + origin[r][0]
         return remote(
-            send_back.at[g, p], got_back.at[g, p], back_send.at[g, p], back_recv.at[g, p], {"exp": behind(p)}
+            send_back.at[g, here], got_back.at[g, there], back_send.at[g, here], back_recv.at[g, there], source(dy, r)
         )
+
+    def back_wait(g, dy, s):
+        p = dy * nz + s
+        remote(
+            send_back.at[g, p], got_back.at[g, p], back_send.at[g, p], back_recv.at[g, p], worker(dy, s)
+        ).wait_recv()
 
     def expert_half(half):
         r = pl.ds(half * hrows, hrows)
@@ -292,6 +326,9 @@
 
     expert_half(1)
 
+    def return_group(g):
+        chunks(0, ny, lambda dy, r: back_copy(g, dy, r).start())
+
     @pl.loop(0, ngroup)
     def _(g):
         stage[...] = dot_nt(upg[...], w1[cols(g, gw), :])
@@ -300,9 +337,9 @@
         def _(p):
             send_back[g, p] = stage[slots(p), :].astype(BF16)
 
-        @pl.loop(1, nexp)
-        def _(p):
-            back_copy(g, p).start()
+        @pl.when(g < AHEAD)
+        def _():
+            return_group(g)
 
     nblk = nx * 4
     wr1, wr2 = width // nblk, ff // nblk
@@ -402,9 +439,7 @@
         return remote(m, m, delta_send.at[g, k], delta_recv.at[g, k], b_dev(lax.rem(b_me + k, 4)))
 
     def combine(g):
-        @pl.loop(1, nexp)
-        def _(p):
-            back_copy(g, p).wait_recv()
+        chunks(0, ny, functools.partial(back_wait, g))
 
         stage[slots(0), :] = send_back[g, 0].astype(F32)
 
@@ -418,6 +453,11 @@
         g_all[mine, c] = total
         for d in g_sends(g):
             d.start()
+
+        @pl.when(g + AHEAD < ngroup)
+        def _():
+            return_group(g + AHEAD)
+
         prod = total.astype(F32) * att[:, c].astype(F32)
         for i in range(group):
             d = lax.dot_general(
@@ -594,14 +634,15 @@
     for c in outs[3:]:
         c.start()
 
-    @pl.loop(1, nexp)
-    def _(p):
-        a2a(0, p).wait_send()
-        a2a(1, p).wait_send()
+    def sent(dy, n):
+        a2a(0, dy, n).wait_send()
+        a2a(1, dy, n).wait_send()
 
         @pl.loop(0, ngroup)
         def _(g):
-            back_copy(g, p).wait_send()
+            back_copy(g, dy, n).wait_send()
+
+    chunks(0, ny, sent)
 
     for c in q_sends:
         c.wait_send()
@@ -644,7 +685,7 @@
     ff = w_in.shape[2]
     heads = width // HEAD_DIM
     nexp, nctx = lax.axis_size("exp"), lax.axis_size("ctx")
-    nx, ny = nctx // 4, min(4, max(2, nexp // 4))
+    nx, ny = nctx // 4, nexp // 4
     cap = 3 * tok // nexp
     pairs = nexp * cap
     group = 3 if heads % 3 == 0 else 2

time: 151 us -> 134 us (0.89)
  Pallas kernels: 150 us -> 133 us
    pallas_call x1, Pallas kernels: 147 us -> 130 us  [per_device(): pl.pallas_call(functools.partial(kernel, nx, ny, nexp, group), out_shape=...]
where the time goes in v3:
time: 134 us
  Pallas kernels  133 us (99%)
    pallas_call x1, Pallas kernels, per_device(): pl.pallas_call(functools.partial(kernel, nx, ny, nexp, group), out_shape=...  130 us

profile of v3, /device:TPU:1, one launch (start us, length us, event | category | flops | bytes accessed | tf_op | source)
XLA Modules:
  0.0 133.6 jit_solution(10862655839486870377)
XLA Ops:
  0.6 130.5 %block_backward.1 = (bf16[128,1536]{1,0:T(8,128)(2,1)}, bf16[128,1536]{1,0:T(8,128)(2,1)}, bf16[128,1536]{1,0:T(8,128)(2,1)}, bf16[96,768]{1,0:T(8,128)(2,1)}, bf16[48,1536]{1,0:T(8,128)(2,1)}) custom-call(s32[2,128]{1,0:T(2,128)} %bitcast.25, f32[2,128]{1,0:T(2,128)} %bitcast.26, bf16[128,1536]{1,0:T(8,128)(2,1)} %bitcast.20, bf16[128,1536]{1,0:T(8,128)(2,1)} %bitcast.21, ...), custom_call_target="tpu_custom_call" | custom-call | tf_op jit(solution)/shard_map/block_backward/pallas_call | solution.py:725
  131.1 2.5 %hand_out.1 = (bf16[128,1536]{1,0:T(8,128)(2,1)}, bf16[128,1536]{1,0:T(8,128)(2,1)}, bf16[128,1536]{1,0:T(8,128)(2,1)}, bf16[96,768]{1,0:T(8,128)(2,1)}, bf16[48,1536]{1,0:T(8,128)(2,1)}) custom-call(bf16[128,1536]{1,0:T(8,128)(2,1)} %get-tuple-element.15.refs_0_, bf16[128,1536]{1,0:T(8,128)(2,1)} %get-tuple-element.16.refs_1_, ...), custom_call_target="tpu_custom_call" | custom-call | tf_op jit(solution)/shard_map/hand_out/pallas_call | solution.py:739

commit v4 on v3

--- a/solution.py
+++ b/solution.py
@@ -13,6 +13,7 @@
 BF16 = jnp.bfloat16
 LAG = 2
 AHEAD = 2
+EARLY = 1
 
 
 def dot_nn(a, b):
@@ -113,11 +114,14 @@
 
     barrier = pltpu.get_barrier_semaphore()
 
-    def greet(dy, n):
-        for dev in (worker(dy, n), source(dy, n)):
-            pl.semaphore_signal(barrier, inc=1, device_id=dev, device_id_type=MESH)
-
-    chunks(0, ny, greet)
+    def greet(dev):
+        pl.semaphore_signal(barrier, inc=1, device_id=dev, device_id_type=MESH)
+
+    chunks(0, ny, lambda dy, n: greet(worker(dy, n)))
+
+    @pl.loop(0, ny)
+    def _(dy):
+        greet({"exp": owner(dy, 3 - 2 * zl), "ctx": ctx})
 
     @pl.loop(1, nx)
     def _(k):
@@ -139,21 +143,6 @@
     for c in local:
         c.start()
 
-    pl.semaphore_wait(barrier, 2 * (nexp - 1) + nx - 1 + 3)
-    q_sends = [
-        remote(q_ref, blk(q_all, b_me), q_send.at[i], q_recv.at[i], dev) for i, dev in enumerate((sib, zpart))
-    ]
-    for c in q_sends:
-        c.start()
-
-    def kv_copy(which, k):
-        src, buf = ((k_ref, k_all), (v_ref, v_all))[which]
-        return remote(
-            src, blk(buf, my_x), kv_send.at[which, k], kv_recv.at[which, k], x_dev(lax.rem(my_x + k, nx))
-        )
-
-    for k in range(1, nx):
-        kv_copy(0, k).start()
     expert = lax.broadcasted_iota(jnp.int32, (nexp, tok), 0)
     first, second = ids_ref[0:1, :] == expert, ids_ref[1:2, :] == expert
     member = jnp.where(first | second, 1.0, 0.0)
@@ -214,15 +203,35 @@
     def arrived(which, half):
         buffer, got = ((send_rows, got_rows), (send_grads, got_grads))[which]
 
-        def wait(dy, r):
+        def take(dy, r):
             p = dy * nz + r
             remote(buffer.at[p], got.at[p], a2a_send.at[which, p], a2a_recv.at[which, p], source(dy, r)).wait_recv()
-
-        chunks(half * hy, (half + 1) * hy, wait)
+            wide[slots(p), :] = got[p].astype(F32)
+
+        if half == 0:
+            wide[slots(0), :] = got[0].astype(F32)
+        chunks(half * hy, (half + 1) * hy, take)
 
     local[0].wait()
     fill(0, 0)
+    pl.semaphore_wait(barrier, nexp - 1 + ny + nx - 1 + 3)
     send(0, 0)
+
+    q_sends = [
+        remote(q_ref, blk(q_all, b_me), q_send.at[i], q_recv.at[i], dev) for i, dev in enumerate((sib, zpart))
+    ]
+    for c in q_sends:
+        c.start()
+
+    def kv_copy(which, k):
+        src, buf = ((k_ref, k_all), (v_ref, v_all))[which]
+        return remote(
+            src, blk(buf, my_x), kv_send.at[which, k], kv_recv.at[which, k], x_dev(lax.rem(my_x + k, nx))
+        )
+
+    for k in range(1, nx):
+        kv_copy(0, k).start()
+
     local[1].wait()
     fill(1, 0)
     send(1, 0)
@@ -256,17 +265,13 @@
     def expert_half(half):
         r = pl.ds(half * hrows, hrows)
 
-        def unpack(got, out):
-            @pl.loop(half * nhalf, (half + 1) * nhalf)
-            def _(p):
-                wide[slots(p), :] = got[p].astype(F32)
-
+        def unpack(out):
             @tiles(width, wide_tile)
             def _(j):
                 out[r, cols(j, wide_tile)] = wide[r, cols(j, wide_tile)].astype(BF16)
 
         arrived(0, half)
-        unpack(got_rows, rows)
+        unpack(rows)
         if half == 0:
             local[2].wait()
             local[3].wait()
@@ -276,7 +281,14 @@
             upper[:, cols(j, t)] = dot_nn(rows[r, :], w1[:, cols(j, t)])
 
         arrived(1, half)
-        unpack(got_grads, grads)
+
+        if half == 1:
+
+            @pl.loop(0, EARLY)
+            def _(g):
+                return_group(g, 0)
+
+        unpack(grads)
 
         @tiles(ff, t)
         def _(j):
@@ -286,7 +298,55 @@
             d = dot_nt(grads[r, :], w2[cols(j, t), :])
             upg[r, cols(j, t)] = (d * sig * (1.0 + u * (1.0 - sig))).astype(BF16)
 
+    nblk = nx * 4
+    wr1, wr2 = width // nblk, ff // nblk
+
+    def half_term1(half):
+        r = pl.ds(half * hrows, hrows)
+
+        @pl.loop(0, 4)
+        def _(j):
+            term = dot_tn(rows[r, cols(j, width // 4)], upg[r, :])
+            for i in range(nx):
+                part1 = term[i * wr1 : (i + 1) * wr1]
+                at = (i % 2, j * (nx // 2) + i // 2)
+                t1[at] = (part1 + t1[at].astype(F32) if half else part1).astype(BF16)
+
+    def half_term2(half):
+        r = pl.ds(half * hrows, hrows)
+
+        @pl.loop(0, 2)
+        def _(j):
+            term = dot_tn(act[r, cols(j, ff // 2)], grads[r, :])
+            for i in range(2 * nx):
+                part2 = term[i * wr2 : (i + 1) * wr2]
+                at = (i % 2, j * nx + i // 2)
+                t2[at] = (part2 + t2[at].astype(F32) if half else part2).astype(BF16)
+
+    def return_group(g, half):
+        chunks(half * hy, (half + 1) * hy, lambda dy, r: back_copy(g, dy, r).start())
+
+    def row_back(half):
+        r = pl.ds(half * hrows, hrows)
+
+        @pl.loop(0, ngroup)
+        def _(g):
+            stage[r, :] = dot_nt(upg[r, :], w1[cols(g, gw), :])
+
+            @pl.loop(half * nhalf, (half + 1) * nhalf)
+            def _(p):
+                send_back[g, p] = stage[slots(p), :].astype(BF16)
+
+            @pl.when(g < (AHEAD if half else 0))
+            def _():
+                @pl.when(g >= EARLY)
+                def _():
+                    return_group(g, 0)
+
+                return_group(g, half)
+
     expert_half(0)
+    row_back(0)
 
     def q_forward():
         mine = blk(q_all, b_z)
@@ -324,45 +384,22 @@
     for k in range(1, 4):
         sum_copy(k).start()
 
+    half_term1(0)
+    half_term2(0)
+
     expert_half(1)
 
-    def return_group(g):
-        chunks(0, ny, lambda dy, r: back_copy(g, dy, r).start())
-
-    @pl.loop(0, ngroup)
-    def _(g):
-        stage[...] = dot_nt(upg[...], w1[cols(g, gw), :])
-
-        @pl.loop(0, nexp)
-        def _(p):
-            send_back[g, p] = stage[slots(p), :].astype(BF16)
-
-        @pl.when(g < AHEAD)
-        def _():
-            return_group(g)
-
-    nblk = nx * 4
-    wr1, wr2 = width // nblk, ff // nblk
     x_next, x_far, x_prev = (lax.rem(my_x + k, nx) for k in range(1, 4))
     w_pair = (
         remote(t1.at[1 - core], t1_pair, w_send.at[0], w_recv.at[0], sib),
         remote(t2.at[1 - core], t2_pair, w_send.at[1], w_recv.at[1], sib),
     )
 
-    @pl.loop(0, 4)
-    def _(j):
-        term = dot_tn(rows[:, cols(j, width // 4)], upg[...]).astype(BF16)
-        for i in range(nx):
-            t1[i % 2, j * (nx // 2) + i // 2] = term[i * wr1 : (i + 1) * wr1]
-
+    half_term1(1)
     w_pair[0].start()
 
-    @pl.loop(0, 2)
-    def _(j):
-        term = dot_tn(act[:, cols(j, ff // 2)], grads[...]).astype(BF16)
-        for i in range(2 * nx):
-            t2[i % 2, j * nx + i // 2] = term[i * wr2 : (i + 1) * wr2]
-
+    row_back(1)
+    half_term2(1)
     w_pair[1].start()
 
     def w_first(w):
@@ -439,14 +476,13 @@
         return remote(m, m, delta_send.at[g, k], delta_recv.at[g, k], b_dev(lax.rem(b_me + k, 4)))
 
     def combine(g):
-        chunks(0, ny, functools.partial(back_wait, g))
+        def take(dy, n):
+            back_wait(g, dy, n)
+            p = dy * nz + n
+            stage[slots(p), :] = got_back[g, p].astype(F32)
 
         stage[slots(0), :] = send_back[g, 0].astype(F32)
-
-        @pl.loop(1, nexp)
-        def _(p):
-            stage[slots(p), :] = got_back[g, p].astype(F32)
-
+        chunks(0, ny, take)
         back[...] = stage[...].astype(BF16)
         c = cols(g, gw)
         total = (og[:, c].astype(F32) + dot_nn(pick_t[...], back[...])).astype(BF16)
@@ -456,7 +492,11 @@
 
         @pl.when(g + AHEAD < ngroup)
         def _():
-            return_group(g + AHEAD)
+            @pl.when(g + AHEAD >= EARLY)
+            def _():
+                return_group(g + AHEAD, 0)
+
+            return_group(g + AHEAD, 1)
 
         prod = total.astype(F32) * att[:, c].astype(F32)
         for i in range(group):
@@ -570,6 +610,37 @@
         ).astype(BF16)
         far_copy(g).start()
 
+    def first_sent():
+        def sent(dy, n):
+            a2a(0, dy, n).wait_send()
+            a2a(1, dy, n).wait_send()
+
+        chunks(0, ny, sent)
+        for c in q_sends:
+            c.wait_send()
+        q_forward().wait_send()
+        for which in range(2):
+            for k in range(1, nx):
+                kv_copy(which, k).wait_send()
+        for k in range(1, 4):
+            sum_copy(k).wait_send()
+
+    def back_sent(g):
+        chunks(0, ny, lambda dy, n: back_copy(g, dy, n).wait_send())
+
+    def group_sent(g):
+        for c in g_sends(g):
+            c.wait_send()
+        g_forward(g).wait_send()
+        for k in range(1, 4):
+            delta_copy(g, k).wait_send()
+        for c in pair_copies(g):
+            c.wait_send()
+        for w in range(2):
+            for c in x_first(w, g) + x_second(w, g):
+                c.wait_send()
+        far_copy(g).wait_send()
+
     @pl.loop(0, ngroup + LAG)
     def _(step):
         @pl.when((step >= 1) & (step <= ngroup))
@@ -596,15 +667,32 @@
         def _():
             x_relay(step - LAG)
 
+        @pl.when(step == 2)
+        def _():
+            first_sent()
+
         @pl.when(step == ngroup)
         def _():
             w_over_z()
+
+            @pl.loop(0, ngroup)
+            def _(g):
+                back_sent(g)
+
+            for w in range(2):
+                for c in w_first(w) + w_second(w):
+                    c.wait_send()
 
     rows_x = pl.ds(pl.multiple_of(my_x * tok, tok), tok)
 
     @pl.loop(0, ngroup)
     def _(g):
         c = cols(g, gw)
+
+        @pl.when(g > 0)
+        def _():
+            group_sent(g - 1)
+
         far_copy(g).wait_recv()
         dq[mine, c] = (
             dq[mine, c].astype(F32) + dq_pair[zl, :, c].astype(F32) + dq_far[:, c].astype(F32)
@@ -634,41 +722,8 @@
     for c in outs[3:]:
         c.start()
 
-    def sent(dy, n):
-        a2a(0, dy, n).wait_send()
-        a2a(1, dy, n).wait_send()
-
-        @pl.loop(0, ngroup)
-        def _(g):
-            back_copy(g, dy, n).wait_send()
-
-    chunks(0, ny, sent)
-
-    for c in q_sends:
-        c.wait_send()
-    q_forward().wait_send()
-    for which in range(2):
-        for k in range(1, nx):
-            kv_copy(which, k).wait_send()
-    for k in range(1, 4):
-        sum_copy(k).wait_send()
-    for w in range(2):
-        for c in w_first(w) + w_second(w):
-            c.wait_send()
-
-    @pl.loop(0, ngroup)
-    def _(g):
-        for c in g_sends(g):
-            c.wait_send()
-        g_forward(g).wait_send()
-        for k in range(1, 4):
-            delta_copy(g, k).wait_send()
-        for c in pair_copies(g):
-            c.wait_send()
-        for w in range(2):
-            for c in x_first(w, g) + x_second(w, g):
-                c.wait_send()
-        far_copy(g).wait_send()
+    for g in range(ngroup - 1, ngroup):
+        group_sent(g)
 
     for c in outs:
         c.wait()

time: 134 us -> 128 us (0.955)
  Pallas kernels: 133 us -> 126 us
    pallas_call x1, Pallas kernels: 130 us -> 123 us  [per_device(): pl.pallas_call(functools.partial(kernel, nx, ny, nexp, group), out_shape=...]
where the time goes in v4:
time: 128 us; the launch traced here: 127 us
  Pallas kernels  126 us (98%)
    pallas_call x1, Pallas kernels, per_device(): pl.pallas_call(functools.partial(kernel, nx, ny, nexp, group), out_shape=...  123 us

profile of v4, /device:TPU:1, one launch (start us, length us, event | category | flops | bytes accessed | tf_op | source)
XLA Modules:
  0.0 126.6 jit_solution(9461356643523122849)
XLA Ops:
  0.6 123.5 %block_backward.1 = (bf16[128,1536]{1,0:T(8,128)(2,1)}, bf16[128,1536]{1,0:T(8,128)(2,1)}, bf16[128,1536]{1,0:T(8,128)(2,1)}, bf16[96,768]{1,0:T(8,128)(2,1)}, bf16[48,1536]{1,0:T(8,128)(2,1)}) custom-call(s32[2,128]{1,0:T(2,128)} %bitcast.25, f32[2,128]{1,0:T(2,128)} %bitcast.26, bf16[128,1536]{1,0:T(8,128)(2,1)} %bitcast.20, bf16[128,1536]{1,0:T(8,128)(2,1)} %bitcast.21, ...), custom_call_target="tpu_custom_call" | custom-call | tf_op jit(solution)/shard_map/block_backward/pallas_call | solution.py:780
  124.1 2.5 %hand_out.1 = (bf16[128,1536]{1,0:T(8,128)(2,1)}, bf16[128,1536]{1,0:T(8,128)(2,1)}, bf16[128,1536]{1,0:T(8,128)(2,1)}, bf16[96,768]{1,0:T(8,128)(2,1)}, bf16[48,1536]{1,0:T(8,128)(2,1)}) custom-call(bf16[128,1536]{1,0:T(8,128)(2,1)} %get-tuple-element.15.refs_0_, bf16[128,1536]{1,0:T(8,128)(2,1)} %get-tuple-element.16.refs_1_, ...), custom_call_target="tpu_custom_call" | custom-call | tf_op jit(solution)/shard_map/hand_out/pallas_call | solution.py:794

commit v5 on v4

--- a/solution.py
+++ b/solution.py
@@ -399,9 +399,6 @@
     w_pair[0].start()
 
     row_back(1)
-    half_term2(1)
-    w_pair[1].start()
-
     def w_first(w):
         t, land, relay = ((t1, t1_x, t1_relay), (t2, t2_x, t2_relay))[w]
         return [
@@ -422,6 +419,9 @@
         ]
 
     for w, (t, pair) in enumerate(((t1, t1_pair), (t2, t2_pair))):
+        if w == 1:
+            half_term2(1)
+            w_pair[1].start()
         w_pair[w].wait()
 
         @pl.loop(0, 2 * nx)
@@ -487,7 +487,7 @@
         c = cols(g, gw)
         total = (og[:, c].astype(F32) + dot_nn(pick_t[...], back[...])).astype(BF16)
         g_all[mine, c] = total
-        for d in g_sends(g):
+        for d in g_sends(g)[::-1]:
             d.start()
 
         @pl.when(g + AHEAD < ngroup)

time: 128 us -> 128 us (level)
  no operation moved by 1% of the time
where the time goes in v5:
time: 128 us; the launch traced here: 127 us
  Pallas kernels  126 us (98%)
    pallas_call x1, Pallas kernels, per_device(): pl.pallas_call(functools.partial(kernel, nx, ny, nexp, group), out_shape=...  124 us

profile of v5, /device:TPU:1, one launch (start us, length us, event | category | flops | bytes accessed | tf_op | source)
XLA Modules:
  0.0 127.1 jit_solution(13930686328177215750)
XLA Ops:
  0.6 124.0 %block_backward.1 = (bf16[128,1536]{1,0:T(8,128)(2,1)}, bf16[128,1536]{1,0:T(8,128)(2,1)}, bf16[128,1536]{1,0:T(8,128)(2,1)}, bf16[96,768]{1,0:T(8,128)(2,1)}, bf16[48,1536]{1,0:T(8,128)(2,1)}) custom-call(s32[2,128]{1,0:T(2,128)} %bitcast.25, f32[2,128]{1,0:T(2,128)} %bitcast.26, bf16[128,1536]{1,0:T(8,128)(2,1)} %bitcast.20, bf16[128,1536]{1,0:T(8,128)(2,1)} %bitcast.21, ...), custom_call_target="tpu_custom_call" | custom-call | tf_op jit(solution)/shard_map/block_backward/pallas_call | solution.py:780
  124.6 2.5 %hand_out.1 = (bf16[128,1536]{1,0:T(8,128)(2,1)}, bf16[128,1536]{1,0:T(8,128)(2,1)}, bf16[128,1536]{1,0:T(8,128)(2,1)}, bf16[96,768]{1,0:T(8,128)(2,1)}, bf16[48,1536]{1,0:T(8,128)(2,1)}) custom-call(bf16[128,1536]{1,0:T(8,128)(2,1)} %get-tuple-element.15.refs_0_, bf16[128,1536]{1,0:T(8,128)(2,1)} %get-tuple-element.16.refs_1_, ...), custom_call_target="tpu_custom_call" | custom-call | tf_op jit(solution)/shard_map/hand_out/pallas_call | solution.py:794
